TPU v7x, 128 devices: a whole 4x4x4 slice. The times are simulated.
128 devices in a mesh: ctx: 8 (over x_lo, y), tp: 16 (over x_hi, z, core).
Axes of the slice: x: 4 (x_hi: 2, x_lo: 2; x = x_hi * 2 + x_lo), y: 4, z: 4, core: 2. Of those that a mesh axis runs over, the one named last changes fastest.
Arguments:
- span_query: bfloat16 [2048, 1536], P('ctx'), may hold values from -24 to 24
- span_latent: bfloat16 [2048, 576], P('ctx'), may hold values from -24 to 24
- query_up: bfloat16 [1536, 24576], P(None, 'tp'), may hold values from -0.15625 to 0.15625
- key_value_up: bfloat16 [512, 32768], P(None, 'tp'), may hold values from -0.25 to 0.25
- out_weight: bfloat16 [16384, 7168], P('tp'), may hold values from -0.046875 to 0.046875
- owner_rows: int32 [2048], P('ctx'), may hold values from 0 to 63, as said below
- step_query: bfloat16 [64, 1536], P('ctx'), may hold values from -24 to 24
- latent_cache: bfloat16 [64, 512, 576], P('ctx', 'tp'), may hold values from -24 to 24
- cache_lengths: int32 [64], P('ctx'), may hold values from 1 to 512
Outputs:
- span_output: float32 [2048, 7168], P(('ctx', 'tp'))
- step_output: float32 [64, 16384], P('ctx', 'tp')
Inputs may be any that keep to these rules, and one draw needn't show every extreme that they name: `owner_rows`: in every aligned block of 16 tokens at most 4 name rows of one group of 8 consecutive rows, and some group is named by exactly 4 of them.
All inputs are finite; a program needn't handle non-finite values.
Results may differ from a plain program's by a relative error of at most 0.012.
The roundings to bfloat16 on the way count: a program that leaves them out, or rounds other values in their place, can miss the bound.
Values may be sent and summed in bfloat16 or wider, within the bound.
A program may use at most 192 MiB of HBM per device.

v0:
```python
import jax
import jax.numpy as jnp
from jax import lax
from jax.sharding import PartitionSpec as P

KL = 512
RD = 64
NOPE = 128
VD = 128
HEAD_DEV = 8


NEGATIVE = -1e30


def combined_all(part, axis, combine):
    gathered = jax.tree.map(lambda a: lax.all_gather(a, axis), part)

    def take(source):
        return jax.tree.map(lambda a: lax.dynamic_index_in_dim(a, source, 0, False), gathered)

    return lax.fori_loop(
        1, lax.axis_size(axis), lambda source, state: combine(state, take(source)), take(0)
    )


def fold_block(running, query_nope, query_rope, query_pos, key_nope, values, key_rope, score_scale):
    key_count = key_rope.shape[0]
    key_pos = jnp.arange(key_count, dtype=jnp.int32)
    visible = query_pos[:, None] >= key_pos[None, :]
    scores = jnp.einsum("thc,uhc->thu", query_nope, key_nope, preferred_element_type=jnp.float32)
    scores = scores + jnp.einsum(
        "thc,uc->thu", query_rope, key_rope, preferred_element_type=jnp.float32
    )
    scores = jnp.where(visible[:, None, :], scores * score_scale, NEGATIVE)
    run_max, run_sum, run_acc = running
    new_max = jnp.maximum(run_max, jnp.max(scores, axis=-1))
    raised = jnp.where(visible[:, None, :], jnp.exp(scores - new_max[..., None]), 0.0)
    new_sum = jnp.sum(raised, axis=-1)
    added = jnp.einsum(
        "thu,uhc->thc", raised.astype(jnp.bfloat16), values, preferred_element_type=jnp.float32
    )
    return (new_max, new_sum, added)


def combine(first_part, second_part):
    both_max = jnp.maximum(first_part[0], second_part[0])
    first_scale = jnp.exp(first_part[0] - both_max)
    second_scale = jnp.exp(second_part[0] - both_max)
    new_sum = first_part[1] * first_scale + second_part[1] * second_scale
    new_acc = first_part[2] * first_scale[..., None] + second_part[2] * second_scale[..., None]
    return (both_max, new_sum, new_acc)


def body(
    span_query,
    span_latent,
    query_up,
    key_value_up,
    out_weight,
    owner_rows,
    step_query,
    latent_cache,
    cache_lengths,
):
    tokens = span_query.shape[0]
    score_scale = (NOPE + RD) ** (-0.5)
    ctx_index = lax.axis_index("ctx")
    tp_index = lax.axis_index("tp")
    queries = jnp.dot(span_query, query_up, preferred_element_type=jnp.float32).astype(jnp.bfloat16)
    queries = queries.reshape(tokens, HEAD_DEV, NOPE + RD)
    query_nope = queries[..., :NOPE]
    query_rope = queries[..., NOPE:]
    query_pos = ctx_index * tokens + jnp.arange(tokens, dtype=jnp.int32)
    last_pos = ctx_index * tokens + tokens - 1
    start_state = (
        jnp.full((tokens, HEAD_DEV), NEGATIVE, jnp.float32),
        jnp.zeros((tokens, HEAD_DEV), jnp.float32),
        jnp.zeros((tokens, HEAD_DEV, VD), jnp.float32),
    )
    keyval = lax.all_gather(
        jnp.dot(span_latent[:, :KL], key_value_up, preferred_element_type=jnp.float32).astype(
            jnp.bfloat16
        ),
        "ctx",
        axis=0,
        tiled=True,
    )
    key_rope = lax.all_gather(span_latent[:, KL:], "ctx", axis=0, tiled=True)
    shaped = keyval.reshape(keyval.shape[0], HEAD_DEV, NOPE + VD)

    def compute(current):
        return fold_block(
            current,
            query_nope,
            query_rope,
            query_pos,
            shaped[..., :NOPE],
            shaped[..., NOPE:],
            key_rope,
            score_scale,
        )

    folded = lax.cond(jnp.int32(0) <= last_pos, compute, lambda current: current, start_state)
    head_out = (
        (folded[2] / folded[1][..., None]).astype(jnp.bfloat16).reshape(tokens, HEAD_DEV * VD)
    )
    share = tokens // lax.axis_size("tp")
    span_output = lax.psum_scatter(
        jnp.dot(head_out, out_weight, preferred_element_type=jnp.float32),
        "tp",
        scatter_dimension=0,
        tiled=True,
    )
    ctx_count = lax.axis_size("ctx")
    capacity = share // 4
    row_block = step_query.shape[0]
    sending = lax.dynamic_slice_in_dim(span_latent, tp_index * share, share, 0)
    targets = lax.dynamic_slice_in_dim(owner_rows, tp_index * share, share, 0)
    target_shard = targets // row_block
    target_row = targets % row_block
    shard_hits = (target_shard[:, None] == jnp.arange(ctx_count, dtype=jnp.int32)[None, :]).astype(
        jnp.int32
    )
    slot_rank = jnp.sum((jnp.cumsum(shard_hits, axis=0) - shard_hits) * shard_hits, axis=1)
    placing = (shard_hits.T[:, None, :] == 1) & (
        slot_rank[None, None, :] == jnp.arange(capacity, dtype=jnp.int32)[None, :, None]
    )
    send_latent = jnp.einsum(
        "kcs,sd->kcd", placing.astype(jnp.bfloat16), sending, preferred_element_type=jnp.float32
    ).astype(jnp.bfloat16)
    send_rows = (
        jnp.sum(placing.astype(jnp.int32) * (target_row + 1)[None, None, :], axis=-1) - 1
    ).astype(jnp.bfloat16)
    arrived, arrived_rows = (
        lax.all_to_all(send_latent, "ctx", split_axis=0, concat_axis=0, tiled=True),
        lax.all_to_all(send_rows, "ctx", split_axis=0, concat_axis=0, tiled=True),
    )
    arrived = arrived.reshape(ctx_count * capacity, KL + RD)
    arrived_rows = arrived_rows.reshape(ctx_count * capacity).astype(jnp.float32)
    step_heads = jnp.dot(step_query, query_up, preferred_element_type=jnp.float32).astype(
        jnp.bfloat16
    )
    step_heads = step_heads.reshape(row_block, HEAD_DEV, NOPE + RD)
    up_key = key_value_up.reshape(KL, HEAD_DEV, NOPE + VD)
    absorbed = jnp.einsum(
        "bhc,khc->bhk",
        step_heads[..., :NOPE],
        up_key[..., :NOPE],
        preferred_element_type=jnp.float32,
    ).astype(jnp.bfloat16)
    step_key = jnp.concatenate([absorbed, step_heads[..., NOPE:]], axis=-1)
    all_keys = lax.all_gather(step_key, "tp", axis=1, tiled=True)
    cache_count = latent_cache.shape[1]
    cache_pos = tp_index * cache_count + jnp.arange(cache_count, dtype=jnp.int32)
    cache_seen = cache_pos[None, :] < cache_lengths[:, None]
    cache_scores = (
        jnp.einsum("bhk,bpk->bhp", all_keys, latent_cache, preferred_element_type=jnp.float32)
        * score_scale
    )
    cache_scores = jnp.where(cache_seen[:, None, :], cache_scores, NEGATIVE)
    extra_seen = (
        arrived_rows[None, :] == jnp.arange(row_block, dtype=jnp.int32).astype(jnp.float32)[:, None]
    )
    extra_scores = (
        jnp.einsum("bhk,ek->bhe", all_keys, arrived, preferred_element_type=jnp.float32)
        * score_scale
    )
    extra_scores = jnp.where(extra_seen[:, None, :], extra_scores, NEGATIVE)
    part_max = jnp.maximum(jnp.max(cache_scores, axis=-1), jnp.max(extra_scores, axis=-1))
    cache_raise = jnp.where(
        cache_seen[:, None, :], jnp.exp(cache_scores - part_max[..., None]), 0.0
    )
    extra_raise = jnp.where(
        extra_seen[:, None, :], jnp.exp(extra_scores - part_max[..., None]), 0.0
    )
    part_sum = jnp.sum(cache_raise, axis=-1) + jnp.sum(extra_raise, axis=-1)
    part_acc = jnp.einsum(
        "bhp,bpk->bhk",
        cache_raise.astype(jnp.bfloat16),
        latent_cache[..., :KL],
        preferred_element_type=jnp.float32,
    )
    part_acc = part_acc + jnp.einsum(
        "bhe,ek->bhk",
        extra_raise.astype(jnp.bfloat16),
        arrived[:, :KL],
        preferred_element_type=jnp.float32,
    )
    merged = combined_all((part_max, part_sum, part_acc), "tp", combine)
    mixed_sum = lax.dynamic_slice_in_dim(merged[1], tp_index * HEAD_DEV, HEAD_DEV, 1)
    mixed_acc = lax.dynamic_slice_in_dim(merged[2], tp_index * HEAD_DEV, HEAD_DEV, 1)
    mixed = (mixed_acc / mixed_sum[..., None]).astype(jnp.bfloat16)
    step_output = jnp.einsum(
        "bhk,khc->bhc", mixed, up_key[..., NOPE:], preferred_element_type=jnp.float32
    )
    step_output = step_output.reshape(row_block, HEAD_DEV * VD)
    return (span_output, step_output)


def solution(mesh):
    in_specs = (
        P("ctx", None),
        P("ctx", None),
        P(None, "tp"),
        P(None, "tp"),
        P("tp", None),
        P("ctx"),
        P("ctx", None),
        P("ctx", "tp", None),
        P("ctx"),
    )
    out_specs = (P(("ctx", "tp"), None), P("ctx", "tp"))
    return jax.shard_map(body, mesh=mesh, in_specs=in_specs, out_specs=out_specs, check_vma=False)
```

profile of v0, /device:TPU:26, one launch (start us, length us, event | category | flops | bytes accessed | tf_op | source)
XLA Modules:
  0.0 447.9 jit_solution(2909066867843215698)
XLA Ops:
  7.2 3.2 convolution_convert_fusion.2
  10.6 2.5 copy.51
  18.5 5.6 %all-to-all-start = ((bf16[8,1,4]{2,1,0:T(2,128)(2,1)}), bf16[8,1,4]{2,1,0:T(2,128)(2,1)S(1)}, u32[]{:S(2)}, u32[]{:S(2)}) async-start(bf16[8,1,4]{2,1,0:T(2,128)(2,1)} %copy.55), calls=%async_computation.1 | async-start | bytes 8192 | tf_op jit(solution)/shard_map/all_to_all | solution.py:137
  27.2 6.2 %all-to-all-start.1 = ((bf16[8,4,576]{2,1,0:T(4,128)(2,1)}), bf16[8,4,576]{2,1,0:T(4,128)(2,1)S(1)}, u32[]{:S(2)}, u32[]{:S(2)}) async-start(bf16[8,4,576]{2,1,0:T(4,128)(2,1)} %copy.57), calls=%async_computation.2 | async-start | bytes 81920 | tf_op jit(solution)/shard_map/all_to_all | solution.py:136
  33.7 3.2 all-to-all-done.1
  36.9 25.3 %all-gather.9.cloned.1.call-done = bf16[8,128,576]{2,0,1:T(8,128)(2,1)} async-done(((bf16[8,8,576]{2,0,1:T(8,128)(2,1)}), bf16[8,128,576]{2,0,1:T(8,128)(2,1)}) %all-gather.9.cloned.1.call-update) | async-done | bytes 1179664 | tf_op jit(solution)/shard_map/all_gather | solution.py:153
  69.8 29.4 %all_gather.24 = bf16[2048,64]{0,1:T(8,128)(2,1)S(1)} all-gather(bf16[256,64]{0,1:T(8,128)(2,1)S(1)} %slice-done), channel_id=1, replica_groups=mesh['ctx'=8,'tp'=16] {'ctx'}, dimensions={0}, use_global_device_ids=true | all-gather | bytes 294912 | tf_op jit(solution)/shard_map/all_gather | solution.py:89
  99.2 3.8 convolution_convert_fusion.1
  103.0 52.2 %all-gather.7.cloned.1.call-done = bf16[2048,2048]{1,0:T(8,128)(2,1)} async-done(((bf16[256,2048]{1,0:T(8,128)(2,1)}), bf16[2048,2048]{1,0:T(8,128)(2,1)}) %all-gather.7.cloned.1.call-update) | async-done | bytes 8388624 | tf_op jit(solution)/shard_map/all_gather | solution.py:81
  155.1 46.6 %conditional.1 = (f32[256,8]{0,1:T(8,128)S(1)}, f32[256,8,128]{0,2,1:T(8,128)S(1)}) conditional(s32[]{:T(128)} %convert_element_type.79, () %tuple.41, (s32[]{:T(128)}, s32[256]{0:T(256)S(1)}, bf16[2048,2048]{1,0:T(8,128)(2,1)}, bf16[256,1536]{1,0:T(8,128)(2,1)S(1)}, bf16[2048,64]{0,1:T(8,128)(2,1)S(1)}) %tuple.42), branch_computations={%region_0.0_spmd, %region_1.4_spmd} | conditional | flops 2726820096 | bytes 116968464 | solution.py:104
  155.1 12.3 %copy.47 = bf16[2048,2048]{0,1:T(8,128)(2,1)} copy(bf16[2048,2048]{1,0:T(8,128)(2,1)} %get-tuple-element.224) | data formatting | bytes 16777216 | tf_op jit(solution)/shard_map
  167.7 5.4 %fusion.10 = f32[8,2048,256]{2,1,0:T(8,128)S(1)} fusion(bf16[2048,8,256]{0,2,1:T(8,128)(2,1)} %bitcast.63, bf16[256,8,192]{0,2,1:T(8,128)(2,1)S(1)} %bitcast.68), kind=kOutput, calls=%fused_computation.11 | convolution fusion | flops 1073741824 | bytes 21495808 | tf_op jit(solution)/shard_map/cond/branch_1_fun/thc,uhc->thu/dot_general | solution.py:31
  173.5 7.7 %fusion.73 = (f32[256,8]{0,1:T(8,128)S(1)}, f32[256,8,2048]{0,2,1:T(8,128)}) fusion(bf16[2048,64]{0,1:T(8,128)(2,1)S(1)} %get-tuple-element.198, bf16[256,8,192]{0,2,1:T(8,128)(2,1)S(1)} %bitcast.69, f32[8,2048,256]{2,1,0:T(8,128)S(1)} %fusion.10, pred[256,2048]{0,1:T(8,128)(4,1)S(1)} %iota_compare_fusion), kind=kOutput, calls=%fused_computation.98 | convolution fusion | flops 553646080 | bytes 34611200 | tf_op jit(solution)/shard_map/cond/branch_1_fun/thc,uc->thu/dot_general | solution.py:32
  181.2 10.1 %fusion.12 = f32[256,8,128]{2,0,1:T(8,128)} fusion(bf16[2048,8,256]{0,2,1:T(8,128)(2,1)} %bitcast.64, f32[256,8,2048]{0,2,1:T(8,128)} %get-tuple-element.251, f32[256,8]{0,1:T(8,128)S(1)} %broadcast_maximum_fusion, pred[256,2048]{0,1:T(8,128)(4,1)S(1)} %iota_compare_fusion), kind=kOutput, calls=%fused_computation.14 | convolution fusion | flops 1086324736 | bytes 22552576 | tf_op jit(solution)/shard_map/cond/branch_1_fun/thu,uhc->thc/dot_general | solution.py:40
  192.9 8.8 %fusion.3 = f32[256,8]{0,1:T(8,128)S(1)} fusion(f32[256,8,2048]{0,2,1:T(8,128)} %get-tuple-element.251, f32[256,8]{0,1:T(8,128)S(1)} %broadcast_maximum_fusion, pred[256,2048]{0,1:T(8,128)(4,1)S(1)} %iota_compare_fusion), kind=kLoop, calls=%fused_computation.5 | loop fusion | flops 12580864 | bytes 17317888 | tf_op jit(solution)/shard_map/cond/branch_1_fun/reduce_sum | solution.py:39
  201.8 11.7 %fusion.76 = f32[256,7168]{1,0:T(8,128)} fusion(bf16[256,1024]{0,1:T(8,128)(2,1)S(1)} %bitcast.70, bf16[1024,7168]{1,0:T(8,128)(2,1)} %param.17), kind=kOutput, calls=%fused_computation.101 | convolution fusion | flops 3758096384 | bytes 22544384 | tf_op jit(solution)/shard_map/dot_general | solution.py:110
  214.6 24.0 %all-gather.1 = f32[128,128]{1,0:T(8,128)S(1)} all-gather(f32[8,128]{1,0:T(8,128)S(1)} %add.138), channel_id=3, replica_groups=mesh['ctx'=8,'tp'=16] {'tp'}, dimensions={0}, use_global_device_ids=true | all-gather | bytes 69632 | tf_op jit(solution)/shard_map/all_gather | solution.py:17
  238.6 19.8 %all-gather = f32[128,128]{1,0:T(8,128)S(1)} all-gather(f32[8,128]{1,0:T(8,128)S(1)} %max.27), channel_id=2, replica_groups=mesh['ctx'=8,'tp'=16] {'tp'}, dimensions={0}, use_global_device_ids=true | all-gather | bytes 69632 | tf_op jit(solution)/shard_map/all_gather | solution.py:17
  258.4 86.5 %all-gather.11.cloned.1.call-done = f32[128,128,512]{2,1,0:T(8,128)} async-done(((f32[8,128,512]{2,1,0:T(8,128)}), f32[128,128,512]{2,1,0:T(8,128)}) %all-gather.11.cloned.1.call-update) | async-done | bytes 33554448 | tf_op jit(solution)/shard_map/all_gather | solution.py:17
  346.7 34.5 %while.19 = (s32[]{:T(128)}, f32[8,128]{1,0:T(8,128)S(1)}, f32[8,128]{1,0:T(8,128)S(1)}, f32[8,128,512]{2,1,0:T(8,128)S(1)}, f32[16,8,128]{2,1,0:T(8,128)S(1)}, ...) while((s32[]{:T(128)}, f32[8,128]{1,0:T(8,128)S(1)}, ...), condition=%wide.region_13.14_spmd, body=%wide.region_12.13_spmd.sunk | while | flops 1579013 | bytes 6332567 | solution.py:22
  346.7 2.2 fusion.89
  351.2 2.2 fusion.89
  355.6 2.2 fusion.89
  357.9 2.4 fusion.89
  360.3 2.3 fusion.89
  362.7 2.4 fusion.89
  365.1 2.4 fusion.89
  367.5 2.3 fusion.89
  369.9 2.4 fusion.89
  372.3 2.2 fusion.89
  381.4 2.3 convolution_bitcast_fusion
  383.6 57.7 %reduce-scatter.2.cloned.1.call-done = f32[16,7168]{1,0:T(8,128)} async-done(((f32[256,7168]{1,0:T(8,128)}), f32[16,7168]{1,0:T(8,128)}) %reduce-scatter.2.cloned.1.call-update) | async-done | bytes 458768 | tf_op jit(solution)/shard_map/reduce_scatter | solution.py:109
  (93 shorter events, 32.8 us)
Async XLA Ops:
  7.2 92.0 %copy-start = (bf16[256,1536]{1,0:T(8,128)(2,1)S(1)}, bf16[256,1536]{1,0:T(8,128)(2,1)}, u32[]{:S(2)}) copy-start(bf16[256,1536]{1,0:T(8,128)(2,1)} %param.13) | copy-start | bytes 2359300
  7.2 3.4 copy-start.2
  7.2 8.2 %copy-start.3 = (bf16[256,576]{0,1:T(8,128)(2,1)S(1)}, bf16[256,576]{0,1:T(8,128)(2,1)}, u32[]{:S(2)}) copy-start(bf16[256,576]{0,1:T(8,128)(2,1)} %param.14) | copy-start | bytes 884740
  7.2 55.0 %all-gather.9.cloned.1.call-start = ((), (), s32[]{:S(2)}) async-start(), calls=%async_computation.5 | async-start | bytes 1392640 | tf_op jit(solution)/shard_map/all_gather | solution.py:153
  10.6 6.6 %copy-start.6 = (s32[256]{0:T(256)S(1)}, s32[256]{0:T(256)}, u32[]{:S(2)}) copy-start(s32[256]{0:T(256)} %param.18) | copy-start | bytes 3076
  10.6 13.5 %copy-start.7 = (s32[8]{0:T(128)S(1)}, s32[8]{0:T(128)}, u32[]{:S(2)}) copy-start(s32[8]{0:T(128)} %param.21) | copy-start | bytes 100
  15.3 139.8 %all-gather.7.cloned.1.call-start = ((), (), s32[]{:S(2)}) async-start(), calls=%async_computation.3 | async-start | bytes 9437184 | tf_op jit(solution)/shard_map/all_gather | solution.py:81
  18.5 8.7 %all-to-all-start = ((bf16[8,1,4]{2,1,0:T(2,128)(2,1)}), bf16[8,1,4]{2,1,0:T(2,128)(2,1)S(1)}, u32[]{:S(2)}, u32[]{:S(2)}) async-start(bf16[8,1,4]{2,1,0:T(2,128)(2,1)} %copy.55), calls=%async_computation.1 | async-start | bytes 8192 | tf_op jit(solution)/shard_map/all_to_all | solution.py:137
  27.2 9.6 %all-to-all-start.1 = ((bf16[8,4,576]{2,1,0:T(4,128)(2,1)}), bf16[8,4,576]{2,1,0:T(4,128)(2,1)S(1)}, u32[]{:S(2)}, u32[]{:S(2)}) async-start(bf16[8,4,576]{2,1,0:T(4,128)(2,1)} %copy.57), calls=%async_computation.2 | async-start | bytes 81920 | tf_op jit(solution)/shard_map/all_to_all | solution.py:136
  33.5 311.3 %all-gather.11.cloned.1.call-start = ((), (), s32[]{:S(2)}) async-start(), calls=%async_computation.6 | async-start | bytes 35651584 | tf_op jit(solution)/shard_map/all_gather | solution.py:17
  66.0 3.7 copy-start.4
  66.1 3.7 slice-start
  69.7 371.6 %reduce-scatter.2.cloned.1.call-start = ((), (), s32[]{:S(2)}) async-start(), calls=%async_computation.4 | async-start | bytes 7798784 | tf_op jit(solution)/shard_map/reduce_scatter | solution.py:109
  213.5 0.9 copy-start.5
  381.2 60.2 %copy-start.1 = (bf16[256,1536]{1,0:T(8,128)(2,1)S(1)}, bf16[256,1536]{1,0:T(8,128)(2,1)}, u32[]{:S(2)}) copy-start(bf16[256,1536]{1,0:T(8,128)(2,1)} %param.13) | copy-start | bytes 2359300
Sparse Core Ops, SparseCore 0:
  15.4 46.7 all-gather.8
  63.9 91.2 all-gather.6
  157.6 187.1 all-gather.10
  349.5 91.7 reduce-scatter.1
where the time goes:
time: 451 us; the launch traced here: 448 us
  waiting for transfers between devices  227 us (50%)
  blocking collectives  73.2 us (16%)
  matrix products  55 us (12%)
  other arithmetic  45 us (10%)
  local copies, waits for them, and re-layouts  21.2 us (5%)
  between operations  14 us (3%)
  starting transfers between devices  12 us (3%)
    all_gather x1, waiting for transfers between devices, combined_all(): gathered = jax.tree.map(lambda a: lax.all_gather(a, axis), part)  86.5 us
    reduce_scatter x1, waiting for transfers between devices, body(): lax.psum_scatter(jnp.dot(head_out, out_weight, preferred_element_type=jnp...  57.7 us
    all_gather x1, waiting for transfers between devices, body(): lax.all_gather(jnp.dot(span_latent[:, :KL], key_value_up, preferred_eleme...  52.2 us
    all_gather x2, blocking collectives, combined_all(): gathered = jax.tree.map(lambda a: lax.all_gather(a, axis), part)  43.8 us
    add x15, other arithmetic, combine(): first_part[2] * first_scale[..., None]  33.7 us
    all_gather x1, blocking collectives, body(): key_rope = lax.all_gather(span_latent[:, KL:], 'ctx', axis=0, tiled=True)  29.4 us
    all_gather x1, waiting for transfers between devices, body(): all_keys = lax.all_gather(step_key, 'tp', axis=1, tiled=True)  25.3 us
    another operation x2, local copies, waits for them, and re-layouts  12.6 us
  transfers between devices with their start and end apart: 6, of which 6 were waited for; matrix products, arithmetic and copies ran while one was open for 25% of the time, Pallas kernels for 0%

commit v1 on v0

v1 whole, which is shorter than its diff:
```python
import math

import jax
import jax.numpy as jnp
from jax import lax
from jax.experimental import pallas as pl
from jax.experimental.pallas import tpu as pltpu
from jax.sharding import PartitionSpec as P

KL = 512
RD = 64
NOPE = 128
VD = 128
HD = 8
TOK = 256
LAT = 640
ROWB = 8
CPOS = 32
QL = 1536
D = 7168
NCTX = 8
NTP = 16
CHIPS = 8
NCH = 7
CW = D // NCH
SH = 16
NEGATIVE = -1e30
EXP_SCALE = (NOPE + RD) ** -0.5 * math.log2(math.e)
MESH = pl.DeviceIdType.MESH
F32 = jnp.float32
BF16 = jnp.bfloat16


def dot(a, b):
    return jnp.dot(a, b, preferred_element_type=F32)


def dot_t(a, b):
    return lax.dot_general(a, b, (((1,), (1,)), ((), ())), preferred_element_type=F32)


def iota(shape, dim):
    return lax.broadcasted_iota(jnp.int32, shape, dim)


def split_pair(y):
    rows = y.shape[0]
    low = iota((rows, 128), 1) < 64
    first, middle, last = y[:, :128], y[:, 128:256], y[:, 256:384]
    middle_turned = pltpu.roll(middle, 64, 1)
    last_turned = pltpu.roll(last, 64, 1)
    zero = jnp.zeros_like(first)
    return (
        (first, jnp.where(low, middle, zero)),
        (jnp.where(low, middle_turned, last_turned), jnp.where(low, last_turned, zero)),
    )


def kernel(
    lat_in, xq_in, wq_in, kv_in, wo_in, sq_ref, cache_in, len_ref,
    out_ref, step_ref,
    lat, ext, xq, wq, kvup, wo, cache, q, run_max, run_sum, run_acc, head_out,
    keys, acc_send, acc_recv, ml_send, ml_recv,
    pair_send, own, pair_recv, stage, rs,
    load_sem, wq_sem, wo_sem, xq_sem,
    lat_s, lat_r, rel_s, rel_r, ext_s, ext_r, key_s, key_r,
    acc_s, acc_r, ml_s, ml_r, pair_s, pair_r, rs_s, rs_r,
):
    c = lax.axis_index("ctx")
    t = lax.axis_index("tp")
    core = t % 2
    chip = t // 2
    sibling = {"ctx": c, "tp": t + 1 - 2 * core}

    def remote(src, dst, send, recv, device):
        return pltpu.make_async_remote_copy(
            src_ref=src, dst_ref=dst, send_sem=send, recv_sem=recv, device_id=device, device_id_type=MESH
        )

    barrier = pltpu.get_barrier_semaphore()
    for d in range(1, NCTX):
        pl.semaphore_signal(barrier, inc=1, device_id={"ctx": (c + d) % NCTX, "tp": t}, device_id_type=MESH)
    for d in range(1, NTP):
        pl.semaphore_signal(barrier, inc=1, device_id={"ctx": c, "tp": (t + d) % NTP}, device_id_type=MESH)

    lat_load = pltpu.make_async_copy(lat_in, lat.at[c], load_sem.at[0])
    lat_load.start()
    wq_loads = [
        pltpu.make_async_copy(wq_in.at[:, pl.ds(768 * n, 768)], wq.at[n], wq_sem.at[n]) for n in range(2)
    ]
    for load in wq_loads:
        load.start()
    kv_load = pltpu.make_async_copy(kv_in, kvup, load_sem.at[1])
    kv_load.start()
    xq_loads = []
    for part in range(2):
        for n in range(CHIPS):
            parity = 1 - core if part == 0 else core
            row = pl.multiple_of((2 * n + parity) * SH, SH)
            xq_loads.append(
                pltpu.make_async_copy(
                    xq_in.at[pl.ds(row, SH)], xq.at[pl.ds((part * CHIPS + n) * SH, SH)], xq_sem.at[part * CHIPS + n]
                )
            )
    for load in xq_loads:
        load.start()
    cache_load = pltpu.make_async_copy(cache_in, cache, load_sem.at[2])
    cache_load.start()

    lat_load.wait()
    pl.semaphore_wait(barrier, NCTX - 1 + NTP - 1)

    half = pl.ds(pl.multiple_of(core * 128, 128), 128)
    other_half = pl.ds(pl.multiple_of((1 - core) * 128, 128), 128)
    handoff = pl.ds(pl.multiple_of(t * SH, SH), SH)

    def lat_copy(source, target):
        return remote(
            lat.at[source, half], lat.at[source, half], lat_s.at[target], lat_r.at[source], {"ctx": target, "tp": t}
        )

    def ext_copy(source, target):
        return remote(lat.at[c, handoff], ext.at[source], ext_s.at[target], ext_r.at[source], {"ctx": target, "tp": t})

    def relay_copy(source):
        return remote(lat.at[source, half], lat.at[source, half], rel_s.at[source], rel_r.at[source], sibling)

    def relay_arrival(source):
        return remote(
            lat.at[source, other_half], lat.at[source, other_half], rel_s.at[source], rel_r.at[source], sibling
        )

    def send_latents(n, carry):
        target = NCTX - 1 - n

        @pl.when(target > c)
        def _():
            lat_copy(c, target).start()

        return carry

    lax.fori_loop(0, NCTX, send_latents, 0)

    def send_handoff(n, carry):
        @pl.when(n != c)
        def _():
            ext_copy(c, n).start()

        return carry

    lax.fori_loop(0, NCTX, send_handoff, 0)
    ext[c] = lat[c, handoff]

    step_query = sq_ref[...]
    nopes, ropes = [], []
    for n in range(2):
        wq_loads[n].wait()
        y = dot(step_query, wq[n]).astype(BF16).astype(F32)
        for m in range(2):
            for nope, rope in split_pair(y[:, 384 * m : 384 * (m + 1)]):
                nopes.append(nope)
                ropes.append(rope)
    kv_load.wait()
    absorbed = jnp.concatenate(
        [dot_t(nopes[h].astype(BF16), kvup[:, 256 * h : 256 * h + 128]) for h in range(HD)], axis=0
    )
    keys[t, :, :KL] = absorbed.astype(BF16)
    keys[t, :, KL:] = jnp.concatenate(ropes, axis=0).astype(BF16)

    def key_copy(other):
        return remote(
            keys.at[t], keys.at[t], key_s.at[other], key_r.at[t], {"ctx": c, "tp": 2 * other + core}
        )

    def key_arrival(other):
        source = 2 * other + core
        return remote(keys.at[source], keys.at[source], key_s.at[other], key_r.at[source], sibling)

    def key_relay(other):
        source = 2 * other + core
        return remote(keys.at[source], keys.at[source], key_s.at[CHIPS + other], key_r.at[source], sibling)

    def key_relay_arrival(other):
        source = 2 * other + 1 - core
        return remote(keys.at[source], keys.at[source], key_s.at[CHIPS + other], key_r.at[source], sibling)

    for d in range(1, CHIPS):
        key_copy((chip + d) % CHIPS).start()
    key_relay(chip).start()

    wo_loads = [
        pltpu.make_async_copy(wo_in.at[:, pl.ds(CW * n, CW)], wo.at[n], wo_sem.at[n]) for n in range(NCH)
    ]
    for load in wo_loads:
        load.start()

    for load in xq_loads:
        load.wait()
    for n in range(2):
        y = dot(xq[...], wq[n])
        for m in range(2):
            for e, (nope, rope) in enumerate(split_pair(y[:, 384 * m : 384 * (m + 1)])):
                q[4 * n + 2 * m + e, :, :128] = nope.astype(BF16)
                q[4 * n + 2 * m + e, :, 128:] = rope.astype(BF16)

    def key_value(block, h):
        kv = dot(lat[block, :, :KL], kvup[:, 256 * h : 256 * (h + 1)]).astype(BF16)
        return jnp.concatenate([kv[:, :128], lat[block, :, KL:]], axis=1), kv[:, 128:]

    row = iota((TOK, TOK), 0)
    parity = jnp.where(row < 128, 1 - core, core)
    position = ((row % 128) // SH) * (2 * SH) + parity * SH + row % SH
    visible = position >= iota((TOK, TOK), 1)
    for h in range(HD):
        key, value = key_value(c, h)
        scores = jnp.where(visible, dot_t(q[h], key), NEGATIVE)
        top = jnp.max(scores, axis=1, keepdims=True)
        raised = jnp.exp2((scores - top) * EXP_SCALE)
        run_max[h] = jnp.broadcast_to(top, (TOK, 128))
        run_sum[h] = raised[:, :128] + raised[:, 128:]
        run_acc[h] = dot(raised.astype(BF16), value)

    def forward(block):
        lat_copy(block, c).wait_recv()
        relay_copy(block).start()

    def fold(block):
        for h in range(HD):
            key, value = key_value(block, h)
            scores = dot_t(q[h], key)
            old = run_max[h]
            top = jnp.maximum(old, jnp.max(scores, axis=1, keepdims=True))
            shrink = jnp.exp2((old - top) * EXP_SCALE)
            raised = jnp.exp2((scores - top[:, :1]) * EXP_SCALE)
            run_max[h] = top
            run_sum[h] = run_sum[h] * shrink + (raised[:, :128] + raised[:, 128:])
            run_acc[h] = run_acc[h] * shrink + dot(raised.astype(BF16), value)

    def relay_keys():
        def one(d, carry):
            other = (chip + d) % CHIPS
            key_arrival(other).wait_recv()
            key_relay(other).start()
            return carry

        lax.fori_loop(1, CHIPS, one, 0)

    def decode():
        def arrivals(n, carry):
            key_relay_arrival(n).wait_recv()

            @pl.when(n != c)
            def _():
                ext_copy(n, c).wait_recv()

            return carry

        lax.fori_loop(0, CHIPS, arrivals, 0)
        cache_load.wait()
        extra = ext[...].reshape(NCTX * SH, LAT)
        column = iota((ROWB, 256), 1)
        length = jnp.zeros((ROWB, 256), jnp.int32)
        for b in range(ROWB):
            length = jnp.where(column // CPOS == b, len_ref[b], length)
        in_cache = (column // CPOS == iota((ROWB, 256), 0)) & (t * CPOS + column % CPOS < length)
        pick = jnp.where(iota((ROWB, 128), 1) == RD, 1.0, 0.0).astype(BF16)
        owner = dot_t(pick, extra[:, KL:])
        named = owner == (ROWB * c + iota((ROWB, 128), 0)).astype(F32)
        bias = jnp.concatenate(
            [jnp.where(in_cache, 0.0, NEGATIVE), jnp.where(named, 0.0, NEGATIVE)], axis=1
        ).astype(F32)
        lane = iota((64, 128), 1)
        sub = iota((64, 128), 0)

        def chunk(g, carry):
            query = keys[pl.ds(4 * g, 4)].reshape(256, LAT)
            scores = jnp.concatenate(
                [
                    dot_t(query[:, :KL], cache[:, :KL]) + dot_t(query[:, KL : KL + RD], cache[:, KL:]),
                    dot_t(query, extra),
                ],
                axis=1,
            )
            scores = (scores.reshape(32, ROWB, 384) * EXP_SCALE + bias[None]).reshape(256, 384)
            top = jnp.max(scores, axis=1, keepdims=True)
            raised = jnp.exp2(scores - top)
            total = jnp.sum(raised, axis=1, keepdims=True)
            weights = raised.astype(BF16)
            mixed = dot(weights[:, :256], cache[:, :KL]) + dot(weights[:, 256:], extra[:, :KL])
            acc_send[pl.ds(4 * g, 4)] = mixed.astype(BF16).reshape(4, 64, KL)
            for n in range(4):
                rows = slice(64 * n, 64 * (n + 1))
                packed = jnp.where(lane == sub, top[rows], 0.0) + jnp.where(lane == sub + 64, total[rows], 0.0)
                ml_send[4 * g + n] = jnp.broadcast_to(jnp.sum(packed, axis=0, keepdims=True), (8, 128))
            return carry

        lax.fori_loop(0, 4, chunk, 0)

        def send(d, carry):
            target = (t + d) % NTP
            acc_copy(target).start()
            ml_copy(target).start()
            return carry

        lax.fori_loop(1, NTP, send, 0)
        acc_recv[t] = acc_send[t]
        ml_recv[t] = ml_send[t]

    def acc_copy(target):
        return remote(
            acc_send.at[target], acc_recv.at[t], acc_s.at[target], acc_r.at[t], {"ctx": c, "tp": target}
        )

    def ml_copy(target):
        return remote(ml_send.at[target], ml_recv.at[t], ml_s.at[target], ml_r.at[t], {"ctx": c, "tp": target})

    def acc_arrival(source):
        return remote(acc_send.at[source], acc_recv.at[source], acc_s.at[source], acc_r.at[source], sibling)

    def ml_arrival(source):
        return remote(ml_send.at[source], ml_recv.at[source], ml_s.at[source], ml_r.at[source], sibling)

    @pl.when(c >= 1)
    def _():
        forward(c - 1)

    def turn(n, carry):
        @pl.when(n < c)
        def _():
            forward(c - n - 1)

        @pl.when(n <= c)
        def _():
            relay_arrival(c - n).wait_recv()
            fold(c - n)

        @pl.when(n == 4)
        def _():
            relay_keys()

        @pl.when(n == 5)
        def _():
            decode()

        return carry

    lax.fori_loop(1, NCTX, turn, 0)

    for h in range(HD):
        total = jnp.sum(run_sum[h], axis=1, keepdims=True)
        head_out[:, 128 * h : 128 * (h + 1)] = (run_acc[h] / total).astype(BF16)

    def pair_copy(n):
        return remote(pair_send.at[n], pair_recv.at[n], pair_s.at[n], pair_r.at[n], sibling)

    def rs_copy(n, other):
        rows = pl.ds(pl.multiple_of(other * SH, SH), SH)
        return remote(
            stage.at[n, rows], rs.at[n, chip], rs_s.at[n, other], rs_r.at[n, chip], {"ctx": c, "tp": 2 * other + core}
        )

    def rs_arrival(n, other):
        rows = pl.ds(pl.multiple_of(other * SH, SH), SH)
        return remote(stage.at[n, rows], rs.at[n, other], rs_s.at[n, other], rs_r.at[n, other], sibling)

    def project(n):
        wo_load = pltpu.make_async_copy(wo_in.at[:, pl.ds(CW * n, CW)], wo.at[n], wo_sem.at[n])
        wo_load.wait()
        for m in range(CW // 256):
            columns = slice(256 * m, 256 * (m + 1))
            y = dot(head_out[...], wo[n, :, columns])
            pair_send[n, :, columns] = y[:128].astype(BF16)
            own[n, :, columns] = y[128:].astype(BF16)
        pair_copy(n).start()

    def spread(n):
        pair_copy(n).wait_recv()
        stage[n] = (own[n].astype(F32) + pair_recv[n].astype(F32)).astype(BF16)

        def one(d, carry):
            rs_copy(n, (chip + d) % CHIPS).start()
            return carry

        lax.fori_loop(1, CHIPS, one, 0)
        rs[n, chip] = stage[n, pl.ds(pl.multiple_of(chip * SH, SH), SH)]

    def column_turn(n, carry):
        @pl.when(n < NCH)
        def _():
            project(n)

        @pl.when(n >= 1)
        def _():
            spread(n - 1)

        return carry

    lax.fori_loop(0, NCH + 1, column_turn, 0)

    def merge_arrivals(d, carry):
        source = (t + d) % NTP
        acc_arrival(source).wait_recv()
        ml_arrival(source).wait_recv()
        return carry

    lax.fori_loop(1, NTP, merge_arrivals, 0)
    lane = iota((64, 128), 1)
    sub = iota((64, 128), 0)
    tops, totals = [], []
    for s in range(NTP):
        packed = jnp.broadcast_to(ml_recv[s, 0:1, :], (64, 128))
        tops.append(jnp.sum(jnp.where(lane == sub, packed, 0.0), axis=1, keepdims=True))
        totals.append(jnp.sum(jnp.where(lane == sub + 64, packed, 0.0), axis=1, keepdims=True))
    top = tops[0]
    for s in range(1, NTP):
        top = jnp.maximum(top, tops[s])
    total = jnp.zeros((64, 1), F32)
    summed = jnp.zeros((64, KL), F32)
    for s in range(NTP):
        weight = jnp.exp2(tops[s] - top)
        total = total + totals[s] * weight
        summed = summed + acc_recv[s].astype(F32) * weight
    mixed = summed / total
    for h in range(HD):
        step_ref[:, 128 * h : 128 * (h + 1)] = dot(
            mixed[ROWB * h : ROWB * (h + 1)].astype(BF16), kvup[:, 256 * h + 128 : 256 * (h + 1)]
        )

    for n in range(NCH):

        def arrive(d, carry, n=n):
            rs_arrival(n, (chip + d) % CHIPS).wait_recv()
            return carry

        lax.fori_loop(1, CHIPS, arrive, 0)
        summed = rs[n, 0].astype(F32)
        for s in range(1, CHIPS):
            summed = summed + rs[n, s].astype(F32)
        out_ref[:, CW * n : CW * (n + 1)] = summed

    def drain_ctx(n, carry):
        @pl.when(n > c)
        def _():
            lat_copy(c, n).wait_send()

        @pl.when(n < c)
        def _():
            relay_copy(n).wait_send()

        @pl.when(n != c)
        def _():
            ext_copy(c, n).wait_send()

        @pl.when(n != chip)
        def _():
            key_copy(n).wait_send()

        key_relay(n).wait_send()
        return carry

    lax.fori_loop(0, NCTX, drain_ctx, 0)

    def drain_tp(d, carry):
        target = (t + d) % NTP
        acc_copy(target).wait_send()
        ml_copy(target).wait_send()
        return carry

    lax.fori_loop(1, NTP, drain_tp, 0)

    def drain_columns(n, carry):
        pair_copy(n).wait_send()

        def one(d, carry):
            rs_copy(n, (chip + d) % CHIPS).wait_send()
            return carry

        return lax.fori_loop(1, CHIPS, one, carry)

    lax.fori_loop(0, NCH, drain_columns, 0)


def body(
    span_query,
    span_latent,
    query_up,
    key_value_up,
    out_weight,
    owner_rows,
    step_query,
    latent_cache,
    cache_lengths,
):
    latent = jnp.concatenate(
        [span_latent, owner_rows[:, None].astype(BF16), jnp.zeros((TOK, LAT - KL - RD - 1), BF16)], axis=1
    )
    dma = pltpu.SemaphoreType.DMA
    vmem = pltpu.VMEM
    anywhere = pl.BlockSpec(memory_space=pl.ANY)
    in_vmem = pl.BlockSpec(memory_space=pltpu.VMEM)
    return pl.pallas_call(
        kernel,
        out_shape=(
            jax.ShapeDtypeStruct((SH, D), F32),
            jax.ShapeDtypeStruct((ROWB, HD * VD), F32),
        ),
        in_specs=[anywhere] * 5 + [in_vmem, anywhere, pl.BlockSpec(memory_space=pltpu.SMEM)],
        out_specs=(in_vmem, in_vmem),
        scratch_shapes=[
            vmem((NCTX, TOK, LAT), BF16),
            vmem((NCTX, SH, LAT), BF16),
            vmem((TOK, QL), BF16),
            vmem((2, QL, 768), BF16),
            vmem((KL, HD * 256), BF16),
            vmem((NCH, HD * VD, CW), BF16),
            vmem((ROWB * CPOS, KL + RD), BF16),
            vmem((HD, TOK, 256), BF16),
            vmem((HD, TOK, 128), F32),
            vmem((HD, TOK, 128), F32),
            vmem((HD, TOK, VD), F32),
            vmem((TOK, HD * VD), BF16),
            vmem((NTP, 64, LAT), BF16),
            vmem((NTP, 64, KL), BF16),
            vmem((NTP, 64, KL), BF16),
            vmem((NTP, 8, 128), F32),
            vmem((NTP, 8, 128), F32),
            vmem((NCH, 128, CW), BF16),
            vmem((NCH, 128, CW), BF16),
            vmem((NCH, 128, CW), BF16),
            vmem((NCH, 128, CW), BF16),
            vmem((NCH, CHIPS, SH, CW), BF16),
            dma((3,)),
            dma((2,)),
            dma((NCH,)),
            dma((2 * CHIPS,)),
            dma((NCTX,)),
            dma((NCTX,)),
            dma((NCTX,)),
            dma((NCTX,)),
            dma((NCTX,)),
            dma((NCTX,)),
            dma((2 * CHIPS,)),
            dma((NTP,)),
            dma((NTP,)),
            dma((NTP,)),
            dma((NTP,)),
            dma((NTP,)),
            dma((NCH,)),
            dma((NCH,)),
            dma((NCH, CHIPS)),
            dma((NCH, CHIPS)),
        ],
        compiler_params=pltpu.CompilerParams(
            collective_id=0, has_side_effects=True, vmem_limit_bytes=60 * 1024 * 1024
        ),
        name="attention",
    )(
        latent,
        span_query,
        query_up,
        key_value_up,
        out_weight,
        step_query,
        latent_cache.reshape(ROWB * CPOS, KL + RD),
        cache_lengths,
    )


def solution(mesh):
    in_specs = (
        P("ctx", None),
        P("ctx", None),
        P(None, "tp"),
        P(None, "tp"),
        P("tp", None),
        P("ctx"),
        P("ctx", None),
        P("ctx", "tp", None),
        P("ctx"),
    )
    out_specs = (P(("ctx", "tp"), None), P("ctx", "tp"))
    return jax.shard_map(body, mesh=mesh, in_specs=in_specs, out_specs=out_specs, check_vma=False)
```

time: 451 us -> 95.5 us (0.21)
  the two profiles are of different devices: /device:TPU:26 before, /device:TPU:3 now
where the time goes in v1:
time: 95.5 us; the launch traced here: 95.2 us
  Pallas kernels  88.5 us (93%)
  local copies, waits for them, and re-layouts  4.53 us (5%)
  other arithmetic  1.5 us (2%)
    pallas_call x1, Pallas kernels, body(): pl.pallas_call(kernel, out_shape=(jax.ShapeDtypeStruct((SH, D), F32), jax...  88.5 us
    unnamed x3, local copies, waits for them, and re-layouts  4.35 us

profile of v1, /device:TPU:3, one launch (start us, length us, event | category | flops | bytes accessed | tf_op | source)
XLA Modules:
  0.0 95.2 jit_solution(5792628346103310376)
XLA Ops:
  0.6 0.7 convert_element_type.6
  1.3 0.1 pad.2.clone
  1.4 0.1 convert_element_type.8
  1.5 1.2 %copy.12 = bf16[256,576]{1,0:T(8,128)(2,1)S(1)} copy(bf16[256,576]{0,1:T(8,128)(2,1)} %param.10) | data formatting | bytes 589824 | tf_op args[1]
  2.7 0.8 maximum_maximum_fusion.lat_in
  3.5 88.5 %attention.1 = (f32[16,7168]{1,0:T(8,128)}, f32[8,1024]{1,0:T(8,128)}) custom-call(bf16[256,640]{1,0:T(8,128)(2,1)} %maximum_maximum_fusion.lat_in, bf16[256,1536]{1,0:T(8,128)(2,1)} %xq_in.1, bf16[1536,1536]{1,0:T(8,128)(2,1)} %wq_in.1, bf16[512,2048]{1,0:T(8,128)(2,1)} %kv_in.1, bf16[1024,7168]{1,0:T(8,128)(2,1)} %wo_in.1, bf16[8,1536]{1,0:T(8,128)(2,1)} %sq_ref.1, ...), custom_call_target="tpu_custom_call" | custom-call | tf_op jit(solution)/shard_map/attention/pallas_call | solution.py:501
  92.0 1.8 %copy.16 = f32[16,7168]{1,0:T(8,128)} copy(f32[16,7168]{1,0:T(8,128)} %get-tuple-element.4) | data formatting | bytes 917504
  93.8 1.4 %copy.17 = f32[8,1024]{1,0:T(8,128)} copy(f32[8,1024]{1,0:T(8,128)} %get-tuple-element.5) | data formatting | bytes 65536
  (1 shorter events, 0.0 us)

commit v2 on v1

v2 whole, which is shorter than its diff:
```python
import math

import jax
import jax.numpy as jnp
from jax import lax
from jax.experimental import pallas as pl
from jax.experimental.pallas import tpu as pltpu
from jax.sharding import PartitionSpec as P

KL = 512
RD = 64
NOPE = 128
VD = 128
HD = 8
TOK = 256
LAT = 640
ROWB = 8
CPOS = 32
QL = 1536
D = 7168
NCTX = 8
NTP = 16
CHIPS = 8
NCH = 7
CW = D // NCH
SH = 16
NEGATIVE = -1e30
EXP_SCALE = (NOPE + RD) ** -0.5 * math.log2(math.e)
MESH = pl.DeviceIdType.MESH
F32 = jnp.float32
BF16 = jnp.bfloat16


def dot(a, b):
    return jnp.dot(a, b, preferred_element_type=F32)


def dot_t(a, b):
    return lax.dot_general(a, b, (((1,), (1,)), ((), ())), preferred_element_type=F32)


def iota(shape, dim):
    return lax.broadcasted_iota(jnp.int32, shape, dim)


def split_pair(y):
    rows = y.shape[0]
    low = iota((rows, 128), 1) < 64
    first, middle, last = y[:, :128], y[:, 128:256], y[:, 256:384]
    middle_turned = pltpu.roll(middle, 64, 1)
    last_turned = pltpu.roll(last, 64, 1)
    zero = jnp.zeros_like(first)
    return (
        (first, jnp.where(low, middle, zero)),
        (jnp.where(low, middle_turned, last_turned), jnp.where(low, last_turned, zero)),
    )


def kernel(
    lat_ref, owner_ref, xq_in, wq_in, kv_in, wo_in, sq_ref, cache_in, len_ref,
    out_ref, step_ref,
    lat, ext, xq, wq, wk, wv, wv_t, wo, cache, q, run_max, run_sum, run_acc, head_out,
    keys, acc_send, acc_recv, ml_send, ml_recv,
    pair_send, own, pair_recv, stage, x_recv, x_sum, z_recv,
    load_sem, kv_sem, wq_sem, wo_sem, xq_sem,
    lat_s, lat_r, rel_s, rel_r, ext_s, ext_r, cache_s, cache_r, key_s, key_r,
    acc_s, acc_r, ml_s, ml_r, pair_s, pair_r, x_s, x_r, z_s, z_r,
):
    c = lax.axis_index("ctx")
    t = lax.axis_index("tp")
    core = t % 2
    chip = t // 2
    sibling = {"ctx": c, "tp": t + 1 - 2 * core}
    across = (t + CHIPS) % NTP

    def remote(src, dst, send, recv, device):
        return pltpu.make_async_remote_copy(
            src_ref=src, dst_ref=dst, send_sem=send, recv_sem=recv, device_id=device, device_id_type=MESH
        )

    barrier = pltpu.get_barrier_semaphore()
    for d in range(1, NCTX):
        pl.semaphore_signal(barrier, inc=1, device_id={"ctx": (c + d) % NCTX, "tp": t}, device_id_type=MESH)
    for d in range(NCTX // 2):
        other_row = (c // 4 * 4 + 4) % NCTX + d
        pl.semaphore_signal(barrier, inc=1, device_id={"ctx": other_row, "tp": across}, device_id_type=MESH)
    for d in range(1, CHIPS):
        pl.semaphore_signal(barrier, inc=1, device_id={"ctx": c, "tp": (t + 2 * d) % NTP}, device_id_type=MESH)
    pl.semaphore_signal(barrier, inc=1, device_id=sibling, device_id_type=MESH)

    wq_loads = [
        pltpu.make_async_copy(wq_in.at[:, pl.ds(768 * n, 768)], wq.at[n], wq_sem.at[n]) for n in range(2)
    ]
    for load in wq_loads:
        load.start()
    kv_loads = []
    for h in range(HD):
        for part, held in enumerate((wk, wv)):
            kv_loads.append(
                pltpu.make_async_copy(
                    kv_in.at[:, pl.ds(256 * h + 128 * part, 128)], held.at[:, pl.ds(128 * h, 128)], kv_sem.at[part, h]
                )
            )
    for load in kv_loads:
        load.start()
    xq_loads = []
    for part in range(2):
        for n in range(CHIPS):
            parity = 1 - core if part == 0 else core
            row = pl.multiple_of((2 * n + parity) * SH, SH)
            xq_loads.append(
                pltpu.make_async_copy(
                    xq_in.at[pl.ds(row, SH)], xq.at[pl.ds((part * CHIPS + n) * SH, SH)], xq_sem.at[part * CHIPS + n]
                )
            )
    for load in xq_loads:
        load.start()
    cache_load = pltpu.make_async_copy(cache_in, cache.at[core], load_sem.at[0])
    cache_load.start()

    owner_row = jnp.broadcast_to(owner_ref[...].astype(F32).reshape(1, TOK), (LAT - KL - RD, TOK))
    owner_row = jnp.where(iota((LAT - KL - RD, TOK), 0) == 0, owner_row, 0.0)
    lat[c] = jnp.concatenate([lat_ref[...].astype(F32), owner_row], axis=0).T.astype(BF16)

    pl.semaphore_wait(barrier, NCTX - 1 + NCTX // 2 + CHIPS - 1 + 1)

    half = pl.ds(pl.multiple_of(core * 128, 128), 128)
    other_half = pl.ds(pl.multiple_of((1 - core) * 128, 128), 128)
    quarters = [pl.ds(pl.multiple_of(core * 128 + 64 * n, 64), 64) for n in range(2)]
    handoff = pl.ds(pl.multiple_of(t * SH, SH), SH)

    def lat_copy(source, target, n):
        tp = t if n == 0 else jnp.where(source // 4 == target // 4, t, across)
        return remote(
            lat.at[source, quarters[n]],
            lat.at[source, quarters[n]],
            lat_s.at[n, target],
            lat_r.at[n, source],
            {"ctx": target, "tp": tp},
        )

    def ext_copy(source, target):
        return remote(
            lat.at[c, handoff], ext.at[core, source], ext_s.at[target], ext_r.at[source], {"ctx": target, "tp": t}
        )

    def ext_relay(whose):
        return remote(ext.at[whose], ext.at[whose], ext_s.at[NCTX], ext_r.at[NCTX], sibling)

    def cache_relay(whose):
        return remote(cache.at[whose], cache.at[whose], cache_s, cache_r, sibling)

    def relay_copy(source):
        return remote(lat.at[source, half], lat.at[source, half], rel_s.at[source], rel_r.at[source], sibling)

    def relay_arrival(source):
        return remote(
            lat.at[source, other_half], lat.at[source, other_half], rel_s.at[source], rel_r.at[source], sibling
        )

    def send_latents(n, carry):
        target = NCTX - 1 - n

        @pl.when(target > c)
        def _():
            lat_copy(c, target, 0).start()
            lat_copy(c, target, 1).start()

        return carry

    lax.fori_loop(0, NCTX, send_latents, 0)

    def send_handoff(n, carry):
        @pl.when(n != c)
        def _():
            ext_copy(c, n).start()

        return carry

    lax.fori_loop(0, NCTX, send_handoff, 0)
    ext[core, c] = lat[c, handoff]
    cache_load.wait()
    cache_relay(core).start()

    step_query = sq_ref[...]
    nopes, ropes = [], []
    for n in range(2):
        wq_loads[n].wait()
        y = dot(step_query, wq[n]).astype(BF16).astype(F32)
        for m in range(2):
            for nope, rope in split_pair(y[:, 384 * m : 384 * (m + 1)]):
                nopes.append(nope)
                ropes.append(rope)
    for load in kv_loads:
        load.wait()
    absorbed = jnp.concatenate(
        [dot_t(nopes[h].astype(BF16), wk[:, 128 * h : 128 * (h + 1)]) for h in range(HD)], axis=0
    )
    keys[chip, :, :KL] = absorbed.astype(BF16)
    keys[chip, :, KL:] = jnp.concatenate(ropes, axis=0).astype(BF16)

    def key_copy(other):
        return remote(
            keys.at[chip], keys.at[chip], key_s.at[other], key_r.at[chip], {"ctx": c, "tp": 2 * other + core}
        )

    def key_arrival(other):
        return remote(keys.at[other], keys.at[other], key_s.at[other], key_r.at[other], sibling)

    for d in range(1, CHIPS):
        key_copy((chip + d) % CHIPS).start()

    wo_loads = [
        pltpu.make_async_copy(wo_in.at[:, pl.ds(CW * n, CW)], wo.at[n], wo_sem.at[n]) for n in range(NCH)
    ]
    for load in wo_loads:
        load.start()

    for load in xq_loads:
        load.wait()
    for n in range(2):
        y = dot(xq[...], wq[n])
        for m in range(2):
            for e, (nope, rope) in enumerate(split_pair(y[:, 384 * m : 384 * (m + 1)])):
                q[4 * n + 2 * m + e, :128] = nope.T.astype(BF16)
                q[4 * n + 2 * m + e, 128:] = rope.T.astype(BF16)

    wv_t[...] = wv[...].T

    column = iota((TOK, TOK), 1)
    parity = jnp.where(column < 128, 1 - core, core)
    position = ((column % 128) // SH) * (2 * SH) + parity * SH + column % SH
    visible = iota((TOK, TOK), 0) <= position

    def fold(block, first):
        latents = lat[block, :, :KL]
        rope = lat[block, :, KL:]
        key = dot(latents, wk[...]).astype(BF16)
        value = dot(wv_t[...], latents.T).astype(BF16)

        def score(h):
            return dot(jnp.concatenate([key[:, 128 * h : 128 * (h + 1)], rope], axis=1), q[h])

        def weigh(h, weights, shrink):
            added = dot(value[128 * h : 128 * (h + 1)], weights)
            if not first:
                added = added + (run_acc[h].reshape(VD // 8, 8, TOK) * shrink[None]).reshape(VD, TOK)
            run_acc[h] = added

        scores = {h: score(h) for h in range(2)}
        late = None
        for h in range(HD):
            if h + 2 < HD:
                scores[h + 2] = score(h + 2)
            if late is not None:
                weigh(*late)
            here = scores.pop(h)
            if first:
                here = jnp.where(visible, here, NEGATIVE)
            here = here.reshape(TOK // 8, 8, TOK)
            top = jnp.max(jnp.max(here, axis=0), axis=0, keepdims=True)
            shrink = None
            if first:
                top = jnp.broadcast_to(top, (8, TOK))
            else:
                old = run_max[h]
                top = jnp.maximum(old, top)
                shrink = jnp.exp2((old - top) * EXP_SCALE)
            raised = jnp.exp2((here - top[None]) * EXP_SCALE)
            total = jnp.sum(raised, axis=0)
            run_max[h] = top
            run_sum[h] = total if first else run_sum[h] * shrink + total
            late = (h, raised.reshape(TOK, TOK).astype(BF16), shrink)
        weigh(*late)

    fold(c, True)

    def forward(block):
        lat_copy(block, c, 0).wait_recv()
        lat_copy(block, c, 1).wait_recv()
        relay_copy(block).start()

    def relay_handoff():
        def one(n, carry):
            @pl.when(n != c)
            def _():
                ext_copy(n, c).wait_recv()

            return carry

        lax.fori_loop(0, NCTX, one, 0)
        ext_relay(core).start()

    def decode():
        def arrivals(d, carry):
            key_arrival((chip + d) % CHIPS).wait_recv()
            return carry

        lax.fori_loop(1, CHIPS, arrivals, 0)
        ext_relay(1 - core).wait_recv()
        cache_relay(1 - core).wait_recv()
        extra = ext[...].reshape(2 * NCTX * SH, LAT)
        cached = cache[...].reshape(2 * ROWB * CPOS, KL + RD)
        shape = (ROWB, 512)
        column = iota(shape, 1)
        length = jnp.zeros(shape, jnp.int32)
        for b in range(ROWB):
            length = jnp.where(column % 256 // CPOS == b, len_ref[b], length)
        place = (2 * chip + column // 256) * CPOS + column % CPOS
        in_cache = (column % 256 // CPOS == iota(shape, 0)) & (place < length)
        pick = jnp.where(iota((ROWB, 128), 1) == RD, 1.0, 0.0).astype(BF16)
        owner = dot_t(pick, extra[:, KL:])
        named = owner == (ROWB * c + iota((ROWB, 256), 0)).astype(F32)
        bias = jnp.concatenate(
            [jnp.where(in_cache, 0.0, NEGATIVE), jnp.where(named, 0.0, NEGATIVE)], axis=1
        ).astype(F32)
        lane = iota((64, 128), 1)
        sub = iota((64, 128), 0)

        def chunk(g):
            query = keys[2 * g : 2 * g + 2].reshape(128, LAT)
            scores = jnp.concatenate(
                [
                    dot_t(query[:, :KL], cached[:, :KL]) + dot_t(query[:, KL : KL + RD], cached[:, KL:]),
                    dot_t(query, extra),
                ],
                axis=1,
            )
            scores = (scores.reshape(16, ROWB, 768) * EXP_SCALE + bias[None]).reshape(128, 768)
            top = jnp.max(scores, axis=1, keepdims=True)
            raised = jnp.exp2(scores - top)
            total = jnp.sum(raised, axis=1, keepdims=True)
            weights = raised.astype(BF16)
            mixed = dot(weights[:, :512], cached[:, :KL]) + dot(weights[:, 512:], extra[:, :KL])
            acc_send[2 * g : 2 * g + 2] = mixed.astype(BF16).reshape(2, 64, KL)
            for n in range(2):
                rows = slice(64 * n, 64 * (n + 1))
                packed = jnp.where(lane == sub, top[rows], 0.0) + jnp.where(lane == sub + 64, total[rows], 0.0)
                ml_send[2 * g + n] = jnp.broadcast_to(jnp.sum(packed, axis=0, keepdims=True), (8, 128))

        for g in range(4):
            chunk(g)

        def send(d, carry):
            target = (chip + d) % CHIPS
            acc_copy(target).start()
            ml_copy(target).start()
            return carry

        lax.fori_loop(1, CHIPS, send, 0)
        acc_recv[chip] = acc_send[chip]
        ml_recv[chip] = ml_send[chip]

    def acc_copy(target):
        return remote(
            acc_send.at[target],
            acc_recv.at[chip],
            acc_s.at[target],
            acc_r.at[chip],
            {"ctx": c, "tp": 2 * target + core},
        )

    def ml_copy(target):
        return remote(
            ml_send.at[target], ml_recv.at[chip], ml_s.at[target], ml_r.at[chip], {"ctx": c, "tp": 2 * target + core}
        )

    def acc_arrival(source):
        return remote(acc_send.at[source], acc_recv.at[source], acc_s.at[source], acc_r.at[source], sibling)

    def ml_arrival(source):
        return remote(ml_send.at[source], ml_recv.at[source], ml_s.at[source], ml_r.at[source], sibling)

    @pl.when(c >= 1)
    def _():
        forward(c - 1)

    def turn(n, carry):
        @pl.when(n < c)
        def _():
            forward(c - n - 1)

        @pl.when(n <= c)
        def _():
            relay_arrival(c - n).wait_recv()
            fold(c - n, False)

        @pl.when(n == 4)
        def _():
            relay_handoff()

        @pl.when(n == 5)
        def _():
            decode()

        return carry

    lax.fori_loop(1, NCTX, turn, 0)

    for h in range(HD):
        total = jnp.sum(run_sum[h], axis=0, keepdims=True)
        head_out[:, 128 * h : 128 * (h + 1)] = (run_acc[h] / total).T.astype(BF16)

    def pair_copy(n):
        return remote(pair_send.at[n], pair_recv.at[n], pair_s.at[n], pair_r.at[n], sibling)

    x_hi = chip // 4
    z = chip % 4
    here_rows = pl.ds(pl.multiple_of(x_hi * 64, 64), 64)
    there_rows = pl.ds(pl.multiple_of(64 - x_hi * 64, 64), 64)

    def x_copy(n):
        return remote(stage.at[n, there_rows], x_recv.at[n], x_s.at[n], x_r.at[n], {"ctx": c, "tp": across})

    def z_copy(n, other):
        rows = pl.ds(pl.multiple_of(other * SH, SH), SH)
        return remote(
            x_sum.at[n, rows],
            z_recv.at[n, z],
            z_s.at[n, other],
            z_r.at[n, z],
            {"ctx": c, "tp": 8 * x_hi + 2 * other + core},
        )

    def z_arrival(n, other):
        return remote(z_recv.at[n, other], z_recv.at[n, other], z_s.at[n, other], z_r.at[n, other], sibling)

    def project(n):
        wo_load = pltpu.make_async_copy(wo_in.at[:, pl.ds(CW * n, CW)], wo.at[n], wo_sem.at[n])
        wo_load.wait()
        for m in range(CW // 256):
            columns = slice(256 * m, 256 * (m + 1))
            y = dot(head_out[...], wo[n, :, columns])
            pair_send[n, :, columns] = y[:128].astype(BF16)
            own[n, :, columns] = y[128:].astype(BF16)
        pair_copy(n).start()

    def add_core(n):
        pair_copy(n).wait_recv()
        stage[n] = (own[n].astype(F32) + pair_recv[n].astype(F32)).astype(BF16)
        x_copy(n).start()

    def add_x(n):
        x_copy(n).wait_recv()
        x_sum[n] = (stage[n, here_rows].astype(F32) + x_recv[n].astype(F32)).astype(BF16)
        for d in range(1, 4):
            z_copy(n, (z + d) % 4).start()
        z_recv[n, z] = x_sum[n, pl.ds(pl.multiple_of(z * SH, SH), SH)]

    def column_turn(n, carry):
        @pl.when(n < NCH)
        def _():
            project(n)

        @pl.when((n >= 2) & (n < NCH + 2))
        def _():
            add_core(n - 2)

        @pl.when(n >= 4)
        def _():
            add_x(n - 4)

        return carry

    lax.fori_loop(0, NCH + 4, column_turn, 0)

    def merge_arrivals(d, carry):
        source = (chip + d) % CHIPS
        acc_arrival(source).wait_recv()
        ml_arrival(source).wait_recv()
        return carry

    lax.fori_loop(1, CHIPS, merge_arrivals, 0)
    lane = iota((64, 128), 1)
    sub = iota((64, 128), 0)
    tops, totals = [], []
    for s in range(CHIPS):
        packed = jnp.broadcast_to(ml_recv[s, 0:1, :], (64, 128))
        tops.append(jnp.sum(jnp.where(lane == sub, packed, 0.0), axis=1, keepdims=True))
        totals.append(jnp.sum(jnp.where(lane == sub + 64, packed, 0.0), axis=1, keepdims=True))
    top = tops[0]
    for s in range(1, CHIPS):
        top = jnp.maximum(top, tops[s])
    total = jnp.zeros((64, 1), F32)
    summed = jnp.zeros((64, KL), F32)
    for s in range(CHIPS):
        weight = jnp.exp2(tops[s] - top)
        total = total + totals[s] * weight
        summed = summed + acc_recv[s].astype(F32) * weight
    mixed = summed / total
    for h in range(HD):
        step_ref[:, 128 * h : 128 * (h + 1)] = dot(
            mixed[ROWB * h : ROWB * (h + 1)].astype(BF16), wv[:, 128 * h : 128 * (h + 1)]
        )

    for n in range(NCH):
        for d in range(1, 4):
            z_arrival(n, (z + d) % 4).wait_recv()
        summed = z_recv[n, 0].astype(F32)
        for other in range(1, 4):
            summed = summed + z_recv[n, other].astype(F32)
        out_ref[:, CW * n : CW * (n + 1)] = summed

    def drain_ctx(n, carry):
        @pl.when(n > c)
        def _():
            lat_copy(c, n, 0).wait_send()
            lat_copy(c, n, 1).wait_send()

        @pl.when(n < c)
        def _():
            relay_copy(n).wait_send()

        @pl.when(n != c)
        def _():
            ext_copy(c, n).wait_send()

        @pl.when(n != chip)
        def _():
            key_copy(n).wait_send()
            acc_copy(n).wait_send()
            ml_copy(n).wait_send()

        return carry

    lax.fori_loop(0, NCTX, drain_ctx, 0)

    ext_relay(core).wait_send()
    cache_relay(core).wait_send()

    def drain_columns(n, carry):
        pair_copy(n).wait_send()
        x_copy(n).wait_send()
        for d in range(1, 4):
            z_copy(n, (z + d) % 4).wait_send()
        return carry

    lax.fori_loop(0, NCH, drain_columns, 0)


def body(
    span_query,
    span_latent,
    query_up,
    key_value_up,
    out_weight,
    owner_rows,
    step_query,
    latent_cache,
    cache_lengths,
):
    dma = pltpu.SemaphoreType.DMA
    vmem = pltpu.VMEM
    anywhere = pl.BlockSpec(memory_space=pl.ANY)
    in_vmem = pl.BlockSpec(memory_space=pltpu.VMEM)
    return pl.pallas_call(
        kernel,
        out_shape=(
            jax.ShapeDtypeStruct((SH, D), F32),
            jax.ShapeDtypeStruct((ROWB, HD * VD), F32),
        ),
        in_specs=[in_vmem] * 2 + [anywhere] * 4 + [in_vmem, anywhere, pl.BlockSpec(memory_space=pltpu.SMEM)],
        out_specs=(in_vmem, in_vmem),
        scratch_shapes=[
            vmem((NCTX, TOK, LAT), BF16),
            vmem((2, NCTX, SH, LAT), BF16),
            vmem((TOK, QL), BF16),
            vmem((2, QL, 768), BF16),
            vmem((KL, HD * NOPE), BF16),
            vmem((KL, HD * VD), BF16),
            vmem((HD * VD, KL), BF16),
            vmem((NCH, HD * VD, CW), BF16),
            vmem((2, ROWB * CPOS, KL + RD), BF16),
            vmem((HD, TOK, 256), BF16),
            vmem((HD, 8, TOK), F32),
            vmem((HD, 8, TOK), F32),
            vmem((HD, VD, TOK), F32),
            vmem((TOK, HD * VD), BF16),
            vmem((CHIPS, 64, LAT), BF16),
            vmem((CHIPS, 64, KL), BF16),
            vmem((CHIPS, 64, KL), BF16),
            vmem((CHIPS, 8, 128), F32),
            vmem((CHIPS, 8, 128), F32),
            vmem((NCH, 128, CW), BF16),
            vmem((NCH, 128, CW), BF16),
            vmem((NCH, 128, CW), BF16),
            vmem((NCH, 128, CW), BF16),
            vmem((NCH, 64, CW), BF16),
            vmem((NCH, 64, CW), BF16),
            vmem((NCH, 4, SH, CW), BF16),
            dma((1,)),
            dma((2, HD)),
            dma((2,)),
            dma((NCH,)),
            dma((2 * CHIPS,)),
            dma((2, NCTX)),
            dma((2, NCTX)),
            dma((NCTX,)),
            dma((NCTX,)),
            dma((NCTX + 1,)),
            dma((NCTX + 1,)),
            dma,
            dma,
            dma((CHIPS,)),
            dma((CHIPS,)),
            dma((CHIPS,)),
            dma((CHIPS,)),
            dma((CHIPS,)),
            dma((CHIPS,)),
            dma((NCH,)),
            dma((NCH,)),
            dma((NCH,)),
            dma((NCH,)),
            dma((NCH, 4)),
            dma((NCH, 4)),
        ],
        compiler_params=pltpu.CompilerParams(
            collective_id=0, has_side_effects=True, vmem_limit_bytes=60 * 1024 * 1024
        ),
        name="attention",
    )(
        span_latent.T,
        owner_rows,
        span_query,
        query_up,
        key_value_up,
        out_weight,
        step_query,
        latent_cache.reshape(ROWB * CPOS, KL + RD),
        cache_lengths,
    )


def solution(mesh):
    in_specs = (
        P("ctx", None),
        P("ctx", None),
        P(None, "tp"),
        P(None, "tp"),
        P("tp", None),
        P("ctx"),
        P("ctx", None),
        P("ctx", "tp", None),
        P("ctx"),
    )
    out_specs = (P(("ctx", "tp"), None), P("ctx", "tp"))
    return jax.shard_map(body, mesh=mesh, in_specs=in_specs, out_specs=out_specs, check_vma=False)
```

time: 95.5 us -> 76.7 us (0.80)
  the two profiles are of different devices: /device:TPU:3 before, /device:TPU:10 now
where the time goes in v2:
time: 76.7 us; the launch traced here: 76.5 us
  Pallas kernels  72.7 us (95%)
  local copies, waits for them, and re-layouts  3.19 us (4%)
    pallas_call x1, Pallas kernels, body(): pl.pallas_call(kernel, out_shape=(jax.ShapeDtypeStruct((SH, D), F32), jax...  72.7 us
    unnamed x2, local copies, waits for them, and re-layouts  3.19 us

profile of v2, /device:TPU:10, one launch (start us, length us, event | category | flops | bytes accessed | tf_op | source)
XLA Modules:
  0.0 76.5 jit_solution(14966040923229761757)
XLA Ops:
  0.6 72.7 %attention.1 = (f32[16,7168]{1,0:T(8,128)}, f32[8,1024]{1,0:T(8,128)}) custom-call(bf16[576,256]{1,0:T(8,128)(2,1)} %bitcast.3, s32[256]{0:T(256)} %owner_ref.1, bf16[256,1536]{1,0:T(8,128)(2,1)} %xq_in.1, bf16[1536,1536]{1,0:T(8,128)(2,1)} %wq_in.1, bf16[512,2048]{1,0:T(8,128)(2,1)} %kv_in.1, bf16[1024,7168]{1,0:T(8,128)(2,1)} %wo_in.1, ...), custom_call_target="tpu_custom_call" | custom-call | tf_op jit(solution)/shard_map/attention/pallas_call | solution.py:556
  73.3 1.8 %copy.13 = f32[16,7168]{1,0:T(8,128)} copy(f32[16,7168]{1,0:T(8,128)} %get-tuple-element.4) | data formatting | bytes 917504
  75.1 1.4 %copy.14 = f32[8,1024]{1,0:T(8,128)} copy(f32[8,1024]{1,0:T(8,128)} %get-tuple-element.5) | data formatting | bytes 65536

commit v3 on v2

--- a/solution.py
+++ b/solution.py
@@ -61,9 +61,9 @@
     out_ref, step_ref,
     lat, ext, xq, wq, wk, wv, wv_t, wo, cache, q, run_max, run_sum, run_acc, head_out,
     keys, acc_send, acc_recv, ml_send, ml_recv,
-    pair_send, own, pair_recv, stage, x_recv, x_sum, z_recv,
+    pair_send, own, pair_recv, stage, x_recv, x_sum, z_recv, zz_recv,
     load_sem, kv_sem, wq_sem, wo_sem, xq_sem,
-    lat_s, lat_r, rel_s, rel_r, ext_s, ext_r, cache_s, cache_r, key_s, key_r,
+    lat_s, lat_r, over_s, over_r, rel_s, rel_r, ext_s, ext_r, cache_s, cache_r, key_s, key_r,
     acc_s, acc_r, ml_s, ml_r, pair_s, pair_r, x_s, x_r, z_s, z_r,
 ):
     c = lax.axis_index("ctx")
@@ -72,6 +72,11 @@
     chip = t // 2
     sibling = {"ctx": c, "tp": t + 1 - 2 * core}
     across = (t + CHIPS) % NTP
+    opposite = (chip + 4) % CHIPS
+    x_hi = chip // 4
+    z = chip % 4
+    x_lo = c // 4
+    y = c % 4
 
     def remote(src, dst, send, recv, device):
         return pltpu.make_async_remote_copy(
@@ -81,9 +86,7 @@
     barrier = pltpu.get_barrier_semaphore()
     for d in range(1, NCTX):
         pl.semaphore_signal(barrier, inc=1, device_id={"ctx": (c + d) % NCTX, "tp": t}, device_id_type=MESH)
-    for d in range(NCTX // 2):
-        other_row = (c // 4 * 4 + 4) % NCTX + d
-        pl.semaphore_signal(barrier, inc=1, device_id={"ctx": other_row, "tp": across}, device_id_type=MESH)
+    pl.semaphore_signal(barrier, inc=1, device_id={"ctx": (c + 4) % NCTX, "tp": across}, device_id_type=MESH)
     for d in range(1, CHIPS):
         pl.semaphore_signal(barrier, inc=1, device_id={"ctx": c, "tp": (t + 2 * d) % NTP}, device_id_type=MESH)
     pl.semaphore_signal(barrier, inc=1, device_id=sibling, device_id_type=MESH)
@@ -122,21 +125,25 @@
     owner_row = jnp.where(iota((LAT - KL - RD, TOK), 0) == 0, owner_row, 0.0)
     lat[c] = jnp.concatenate([lat_ref[...].astype(F32), owner_row], axis=0).T.astype(BF16)
 
-    pl.semaphore_wait(barrier, NCTX - 1 + NCTX // 2 + CHIPS - 1 + 1)
+    pl.semaphore_wait(barrier, NCTX - 1 + 1 + CHIPS - 1 + 1)
 
     half = pl.ds(pl.multiple_of(core * 128, 128), 128)
     other_half = pl.ds(pl.multiple_of((1 - core) * 128, 128), 128)
     quarters = [pl.ds(pl.multiple_of(core * 128 + 64 * n, 64), 64) for n in range(2)]
     handoff = pl.ds(pl.multiple_of(t * SH, SH), SH)
 
-    def lat_copy(source, target, n):
-        tp = t if n == 0 else jnp.where(source // 4 == target // 4, t, across)
+    def y_copy(block, target):
         return remote(
-            lat.at[source, quarters[n]],
-            lat.at[source, quarters[n]],
-            lat_s.at[n, target],
-            lat_r.at[n, source],
-            {"ctx": target, "tp": tp},
+            lat.at[block, half], lat.at[block, half], lat_s.at[target], lat_r.at[block], {"ctx": 4 * x_lo + target, "tp": t}
+        )
+
+    def over_copy(block, n):
+        return remote(
+            lat.at[block, quarters[n]],
+            lat.at[block, quarters[n]],
+            over_s.at[n, block],
+            over_r.at[n, block],
+            {"ctx": 4 + y, "tp": (t, across)[n]},
         )
 
     def ext_copy(source, target):
@@ -158,17 +165,17 @@
             lat.at[source, other_half], lat.at[source, other_half], rel_s.at[source], rel_r.at[source], sibling
         )
 
-    def send_latents(n, carry):
-        target = NCTX - 1 - n
-
-        @pl.when(target > c)
-        def _():
-            lat_copy(c, target, 0).start()
-            lat_copy(c, target, 1).start()
-
-        return carry
-
-    lax.fori_loop(0, NCTX, send_latents, 0)
+    @pl.when(x_lo == 0)
+    def _():
+        over_copy(c, 0).start()
+        over_copy(c, 1).start()
+
+    for d in (1, 3, 2):
+        target = (y + d) % 4
+
+        @pl.when((x_lo == 0) | (target > y))
+        def _(target=target):
+            y_copy(c, target).start()
 
     def send_handoff(n, carry):
         @pl.when(n != c)
@@ -177,7 +184,6 @@
 
         return carry
 
-    lax.fori_loop(0, NCTX, send_handoff, 0)
     ext[core, c] = lat[c, handoff]
     cache_load.wait()
     cache_relay(core).start()
@@ -186,9 +192,9 @@
     nopes, ropes = [], []
     for n in range(2):
         wq_loads[n].wait()
-        y = dot(step_query, wq[n]).astype(BF16).astype(F32)
+        up = dot(step_query, wq[n]).astype(BF16).astype(F32)
         for m in range(2):
-            for nope, rope in split_pair(y[:, 384 * m : 384 * (m + 1)]):
+            for nope, rope in split_pair(up[:, 384 * m : 384 * (m + 1)]):
                 nopes.append(nope)
                 ropes.append(rope)
     for load in kv_loads:
@@ -199,16 +205,17 @@
     keys[chip, :, :KL] = absorbed.astype(BF16)
     keys[chip, :, KL:] = jnp.concatenate(ropes, axis=0).astype(BF16)
 
-    def key_copy(other):
-        return remote(
-            keys.at[chip], keys.at[chip], key_s.at[other], key_r.at[chip], {"ctx": c, "tp": 2 * other + core}
-        )
-
-    def key_arrival(other):
-        return remote(keys.at[other], keys.at[other], key_s.at[other], key_r.at[other], sibling)
-
-    for d in range(1, CHIPS):
-        key_copy((chip + d) % CHIPS).start()
+    def key_across(whose):
+        return remote(keys.at[whose], keys.at[whose], key_s.at[0], key_r.at[whose], {"ctx": c, "tp": across})
+
+    def key_copy(whose, d, sem):
+        target = {"ctx": c, "tp": 8 * x_hi + 2 * ((z + d) % 4) + core}
+        return remote(keys.at[whose], keys.at[whose], key_s.at[sem], key_r.at[whose], target)
+
+    key_across(chip).start()
+    for d in (1, 3, 2):
+        key_copy(chip, d, d).start()
+    lax.fori_loop(0, NCTX, send_handoff, 0)
 
     wo_loads = [
         pltpu.make_async_copy(wo_in.at[:, pl.ds(CW * n, CW)], wo.at[n], wo_sem.at[n]) for n in range(NCH)
@@ -216,16 +223,35 @@
     for load in wo_loads:
         load.start()
 
+    def hand_on(d):
+        @pl.when(x_lo == 0)
+        def _():
+            block = (y + d) % 4
+            y_copy(block, y).wait_recv()
+            over_copy(block, 0).start()
+            over_copy(block, 1).start()
+
+            @pl.when(block < c)
+            def _():
+                relay_copy(block).start()
+
+    hand_on(1)
+
     for load in xq_loads:
         load.wait()
     for n in range(2):
-        y = dot(xq[...], wq[n])
+        up = dot(xq[...], wq[n])
         for m in range(2):
-            for e, (nope, rope) in enumerate(split_pair(y[:, 384 * m : 384 * (m + 1)])):
+            for e, (nope, rope) in enumerate(split_pair(up[:, 384 * m : 384 * (m + 1)])):
                 q[4 * n + 2 * m + e, :128] = nope.T.astype(BF16)
                 q[4 * n + 2 * m + e, 128:] = rope.T.astype(BF16)
 
+    hand_on(3)
+    key_across(opposite).wait_recv()
+    for d in (1, 3, 2):
+        key_copy(opposite, d, 3 + d).start()
     wv_t[...] = wv[...].T
+    hand_on(2)
 
     column = iota((TOK, TOK), 1)
     parity = jnp.where(column < 128, 1 - core, core)
@@ -276,8 +302,15 @@
     fold(c, True)
 
     def forward(block):
-        lat_copy(block, c, 0).wait_recv()
-        lat_copy(block, c, 1).wait_recv()
+        @pl.when(block >= 4)
+        def _():
+            y_copy(block, y).wait_recv()
+
+        @pl.when(block < 4)
+        def _():
+            over_copy(block, 0).wait_recv()
+            over_copy(block, 1).wait_recv()
+
         relay_copy(block).start()
 
     def relay_handoff():
@@ -292,11 +325,10 @@
         ext_relay(core).start()
 
     def decode():
-        def arrivals(d, carry):
-            key_arrival((chip + d) % CHIPS).wait_recv()
-            return carry
-
-        lax.fori_loop(1, CHIPS, arrivals, 0)
+        for side in range(2):
+            for d in range(1, 4):
+                whose = 4 * (x_hi if side == 0 else 1 - x_hi) + (z + d) % 4
+                key_copy(whose, d, d).wait_recv()
         ext_relay(1 - core).wait_recv()
         cache_relay(1 - core).wait_recv()
         extra = ext[...].reshape(2 * NCTX * SH, LAT)
@@ -371,19 +403,25 @@
     def ml_arrival(source):
         return remote(ml_send.at[source], ml_recv.at[source], ml_s.at[source], ml_r.at[source], sibling)
 
-    @pl.when(c >= 1)
+    def block_at(n):
+        m = n - y - 1
+        other_ring = (y + m + (m // 2) * (1 - 2 * (m % 2)) + 8) % 4
+        return jnp.where((x_lo == 0) | (n <= y), c - n, other_ring)
+
+    @pl.when(x_lo == 1)
     def _():
-        forward(c - 1)
+        forward(block_at(1))
 
     def turn(n, carry):
-        @pl.when(n < c)
-        def _():
-            forward(c - n - 1)
+        @pl.when((n < c) & (x_lo == 1))
+        def _():
+            forward(block_at(n + 1))
 
         @pl.when(n <= c)
         def _():
-            relay_arrival(c - n).wait_recv()
-            fold(c - n, False)
+            block = block_at(n)
+            relay_arrival(block).wait_recv()
+            fold(block, False)
 
         @pl.when(n == 4)
         def _():
@@ -404,65 +442,100 @@
     def pair_copy(n):
         return remote(pair_send.at[n], pair_recv.at[n], pair_s.at[n], pair_r.at[n], sibling)
 
-    x_hi = chip // 4
-    z = chip % 4
     here_rows = pl.ds(pl.multiple_of(x_hi * 64, 64), 64)
     there_rows = pl.ds(pl.multiple_of(64 - x_hi * 64, 64), 64)
 
+    def row_block(index, count=SH):
+        return pl.ds(pl.multiple_of(index * count, count), count)
+
+    def z_device(other):
+        return {"ctx": c, "tp": 8 * x_hi + 2 * other + core}
+
     def x_copy(n):
         return remote(stage.at[n, there_rows], x_recv.at[n], x_s.at[n], x_r.at[n], {"ctx": c, "tp": across})
 
     def z_copy(n, other):
-        rows = pl.ds(pl.multiple_of(other * SH, SH), SH)
-        return remote(
-            x_sum.at[n, rows],
-            z_recv.at[n, z],
-            z_s.at[n, other],
-            z_r.at[n, z],
-            {"ctx": c, "tp": 8 * x_hi + 2 * other + core},
-        )
+        return remote(x_sum.at[n, row_block(other)], z_recv.at[n, z], z_s.at[n, other], z_r.at[n, z], z_device(other))
 
     def z_arrival(n, other):
         return remote(z_recv.at[n, other], z_recv.at[n, other], z_s.at[n, other], z_r.at[n, other], sibling)
+
+    def first_z_copy(n, other):
+        return remote(
+            stage.at[n, row_block(other, 2 * SH)], zz_recv.at[n, z], z_s.at[n, other], z_r.at[n, z], z_device(other)
+        )
+
+    def first_z_arrival(n, other):
+        return remote(zz_recv.at[n, other], zz_recv.at[n, other], z_s.at[n, other], z_r.at[n, other], sibling)
+
+    def last_x_copy(n):
+        return remote(
+            x_sum.at[n, row_block(1 - x_hi)], x_recv.at[n, :SH], x_s.at[n], x_r.at[n], {"ctx": c, "tp": across}
+        )
 
     def project(n):
         wo_load = pltpu.make_async_copy(wo_in.at[:, pl.ds(CW * n, CW)], wo.at[n], wo_sem.at[n])
         wo_load.wait()
         for m in range(CW // 256):
             columns = slice(256 * m, 256 * (m + 1))
-            y = dot(head_out[...], wo[n, :, columns])
-            pair_send[n, :, columns] = y[:128].astype(BF16)
-            own[n, :, columns] = y[128:].astype(BF16)
+            term = dot(head_out[...], wo[n, :, columns])
+            pair_send[n, :, columns] = term[:128].astype(BF16)
+            own[n, :, columns] = term[128:].astype(BF16)
         pair_copy(n).start()
 
     def add_core(n):
         pair_copy(n).wait_recv()
-        stage[n] = (own[n].astype(F32) + pair_recv[n].astype(F32)).astype(BF16)
-        x_copy(n).start()
-
-    def add_x(n):
-        x_copy(n).wait_recv()
-        x_sum[n] = (stage[n, here_rows].astype(F32) + x_recv[n].astype(F32)).astype(BF16)
-        for d in range(1, 4):
-            z_copy(n, (z + d) % 4).start()
-        z_recv[n, z] = x_sum[n, pl.ds(pl.multiple_of(z * SH, SH), SH)]
+        both = (own[n].astype(F32) + pair_recv[n].astype(F32)).astype(BF16)
+
+        @pl.when(n % 2 == 0)
+        def _():
+            stage[n] = both
+            x_copy(n).start()
+
+        @pl.when(n % 2 == 1)
+        def _():
+            for other in range(4):
+                for side in range(2):
+                    to, of = (2 * other + side) * SH, (4 * side + other) * SH
+                    stage[n, to : to + SH] = both[of : of + SH]
+            for d in (1, 3, 2):
+                first_z_copy(n, (z + d) % 4).start()
+
+    def add_chips(n):
+        @pl.when(n % 2 == 0)
+        def _():
+            x_copy(n).wait_recv()
+            x_sum[n] = (stage[n, here_rows].astype(F32) + x_recv[n].astype(F32)).astype(BF16)
+            for d in (1, 3, 2):
+                z_copy(n, (z + d) % 4).start()
+            z_recv[n, z] = x_sum[n, row_block(z)]
+
+        @pl.when(n % 2 == 1)
+        def _():
+            summed = stage[n, row_block(z, 2 * SH)].astype(F32)
+            for d in (1, 3, 2):
+                other = (z + d) % 4
+                first_z_arrival(n, other).wait_recv()
+                summed = summed + zz_recv[n, other].astype(F32)
+            x_sum[n, : 2 * SH] = summed.astype(BF16)
+            last_x_copy(n).start()
 
     def column_turn(n, carry):
         @pl.when(n < NCH)
         def _():
             project(n)
 
-        @pl.when((n >= 2) & (n < NCH + 2))
-        def _():
-            add_core(n - 2)
-
-        @pl.when(n >= 4)
-        def _():
-            add_x(n - 4)
+        @pl.when((n >= 1) & (n < NCH + 1))
+        def _():
+            add_core(n - 1)
+
+        @pl.when(n >= 3)
+        def _():
+            add_chips(n - 3)
 
         return carry
 
-    lax.fori_loop(0, NCH + 4, column_turn, 0)
+    lax.fori_loop(0, NCH + 3, column_turn, 0)
 
     def merge_arrivals(d, carry):
         source = (chip + d) % CHIPS
@@ -494,19 +567,18 @@
         )
 
     for n in range(NCH):
-        for d in range(1, 4):
-            z_arrival(n, (z + d) % 4).wait_recv()
-        summed = z_recv[n, 0].astype(F32)
-        for other in range(1, 4):
-            summed = summed + z_recv[n, other].astype(F32)
+        if n % 2 == 0:
+            for d in range(1, 4):
+                z_arrival(n, (z + d) % 4).wait_recv()
+            summed = z_recv[n, 0].astype(F32)
+            for other in range(1, 4):
+                summed = summed + z_recv[n, other].astype(F32)
+        else:
+            last_x_copy(n).wait_recv()
+            summed = x_sum[n, row_block(x_hi)].astype(F32) + x_recv[n, :SH].astype(F32)
         out_ref[:, CW * n : CW * (n + 1)] = summed
 
     def drain_ctx(n, carry):
-        @pl.when(n > c)
-        def _():
-            lat_copy(c, n, 0).wait_send()
-            lat_copy(c, n, 1).wait_send()
-
         @pl.when(n < c)
         def _():
             relay_copy(n).wait_send()
@@ -517,7 +589,6 @@
 
         @pl.when(n != chip)
         def _():
-            key_copy(n).wait_send()
             acc_copy(n).wait_send()
             ml_copy(n).wait_send()
 
@@ -525,17 +596,49 @@
 
     lax.fori_loop(0, NCTX, drain_ctx, 0)
 
+    @pl.when(x_lo == 0)
+    def _():
+        for block in range(4):
+            over_copy(block, 0).wait_send()
+            over_copy(block, 1).wait_send()
+
+    for d in (1, 3, 2):
+        target = (y + d) % 4
+
+        @pl.when((x_lo == 0) | (target > y))
+        def _(target=target):
+            y_copy(c, target).wait_send()
+
+    key_across(chip).wait_send()
+    for d in (1, 3, 2):
+        key_copy(chip, d, d).wait_send()
+        key_copy(opposite, d, 3 + d).wait_send()
     ext_relay(core).wait_send()
     cache_relay(core).wait_send()
 
     def drain_columns(n, carry):
         pair_copy(n).wait_send()
-        x_copy(n).wait_send()
-        for d in range(1, 4):
-            z_copy(n, (z + d) % 4).wait_send()
+
+        @pl.when(n % 2 == 0)
+        def _():
+            x_copy(n).wait_send()
+            for d in range(1, 4):
+                z_copy(n, (z + d) % 4).wait_send()
+
+        @pl.when(n % 2 == 1)
+        def _():
+            last_x_copy(n).wait_send()
+            for d in range(1, 4):
+                first_z_copy(n, (z + d) % 4).wait_send()
+
         return carry
 
     lax.fori_loop(0, NCH, drain_columns, 0)
+
+
+def place(span_in, step_in, span_out, step_out):
+    span_out[...] = span_in[...]
+    step_out[...] = step_in[...]
 
 
 def body(
@@ -553,12 +656,13 @@
     vmem = pltpu.VMEM
     anywhere = pl.BlockSpec(memory_space=pl.ANY)
     in_vmem = pl.BlockSpec(memory_space=pltpu.VMEM)
-    return pl.pallas_call(
+    out_shape = (
+        jax.ShapeDtypeStruct((SH, D), F32),
+        jax.ShapeDtypeStruct((ROWB, HD * VD), F32),
+    )
+    results = pl.pallas_call(
         kernel,
-        out_shape=(
-            jax.ShapeDtypeStruct((SH, D), F32),
-            jax.ShapeDtypeStruct((ROWB, HD * VD), F32),
-        ),
+        out_shape=out_shape,
         in_specs=[in_vmem] * 2 + [anywhere] * 4 + [in_vmem, anywhere, pl.BlockSpec(memory_space=pltpu.SMEM)],
         out_specs=(in_vmem, in_vmem),
         scratch_shapes=[
@@ -588,13 +692,16 @@
             vmem((NCH, 64, CW), BF16),
             vmem((NCH, 64, CW), BF16),
             vmem((NCH, 4, SH, CW), BF16),
+            vmem((NCH, 4, 2 * SH, CW), BF16),
             dma((1,)),
             dma((2, HD)),
             dma((2,)),
             dma((NCH,)),
             dma((2 * CHIPS,)),
-            dma((2, NCTX)),
-            dma((2, NCTX)),
+            dma((4,)),
+            dma((NCTX,)),
+            dma((2, 4)),
+            dma((2, 4)),
             dma((NCTX,)),
             dma((NCTX,)),
             dma((NCTX + 1,)),
@@ -629,6 +736,13 @@
         latent_cache.reshape(ROWB * CPOS, KL + RD),
         cache_lengths,
     )
+    return pl.pallas_call(
+        place,
+        out_shape=out_shape,
+        in_specs=[in_vmem] * 2,
+        out_specs=(in_vmem, in_vmem),
+        name="place",
+    )(*results)
 
 
 def solution(mesh):

time: 76.7 us -> 64.1 us (0.84)
  the two profiles are of different devices: /device:TPU:10 before, /device:TPU:6 now
where the time goes in v3:
time: 64.1 us; the launch traced here: 63.9 us
  Pallas kernels  63.3 us (99%)
    pallas_call x1, Pallas kernels, body(): pl.pallas_call(kernel, out_shape=out_shape, in_specs=[in_vmem] * 2 + [any...  61.5 us
    pallas_call x1, Pallas kernels, body(): pl.pallas_call(place, out_shape=out_shape, in_specs=[in_vmem] * 2, out_sp...  1.82 us

profile of v3, /device:TPU:6, one launch (start us, length us, event | category | flops | bytes accessed | tf_op | source)
XLA Modules:
  0.0 63.9 jit_solution(13364473152092593342)
XLA Ops:
  0.6 61.5 %attention.1 = (f32[16,7168]{1,0:T(8,128)}, f32[8,1024]{1,0:T(8,128)}) custom-call(bf16[576,256]{1,0:T(8,128)(2,1)} %bitcast.3, s32[256]{0:T(256)} %owner_ref.1, bf16[256,1536]{1,0:T(8,128)(2,1)} %xq_in.1, bf16[1536,1536]{1,0:T(8,128)(2,1)} %wq_in.1, bf16[512,2048]{1,0:T(8,128)(2,1)} %kv_in.1, bf16[1024,7168]{1,0:T(8,128)(2,1)} %wo_in.1, ...), custom_call_target="tpu_custom_call" | custom-call | tf_op jit(solution)/shard_map/attention/pallas_call | solution.py:663
  62.1 1.8 %place.1 = (f32[16,7168]{1,0:T(8,128)}, f32[8,1024]{1,0:T(8,128)}) custom-call(f32[16,7168]{1,0:T(8,128)} %get-tuple-element.4.span_in, f32[8,1024]{1,0:T(8,128)} %get-tuple-element.5.step_in), custom_call_target="tpu_custom_call" | custom-call | tf_op jit(solution)/shard_map/place/pallas_call | solution.py:739

commit v4 on v3

--- a/solution.py
+++ b/solution.py
@@ -63,7 +63,7 @@
     keys, acc_send, acc_recv, ml_send, ml_recv,
     pair_send, own, pair_recv, stage, x_recv, x_sum, z_recv, zz_recv,
     load_sem, kv_sem, wq_sem, wo_sem, xq_sem,
-    lat_s, lat_r, over_s, over_r, rel_s, rel_r, ext_s, ext_r, cache_s, cache_r, key_s, key_r,
+    lat_s, lat_r, over_s, over_r, rel_s, rel_r, ext_s, ext_r, hand_s, hand_r, cache_s, cache_r, key_s, key_r,
     acc_s, acc_r, ml_s, ml_r, pair_s, pair_r, x_s, x_r, z_s, z_r,
 ):
     c = lax.axis_index("ctx")
@@ -83,6 +83,12 @@
             src_ref=src, dst_ref=dst, send_sem=send, recv_sem=recv, device_id=device, device_id_type=MESH
         )
 
+    wq_loads = [
+        pltpu.make_async_copy(wq_in.at[:, pl.ds(768 * n, 768)], wq.at[n], wq_sem.at[n]) for n in range(2)
+    ]
+    for load in wq_loads:
+        load.start()
+
     barrier = pltpu.get_barrier_semaphore()
     for d in range(1, NCTX):
         pl.semaphore_signal(barrier, inc=1, device_id={"ctx": (c + d) % NCTX, "tp": t}, device_id_type=MESH)
@@ -91,11 +97,67 @@
         pl.semaphore_signal(barrier, inc=1, device_id={"ctx": c, "tp": (t + 2 * d) % NTP}, device_id_type=MESH)
     pl.semaphore_signal(barrier, inc=1, device_id=sibling, device_id_type=MESH)
 
-    wq_loads = [
-        pltpu.make_async_copy(wq_in.at[:, pl.ds(768 * n, 768)], wq.at[n], wq_sem.at[n]) for n in range(2)
-    ]
-    for load in wq_loads:
-        load.start()
+    owner_row = jnp.broadcast_to(owner_ref[...].astype(F32).reshape(1, TOK), (LAT - KL - RD, TOK))
+    owner_row = jnp.where(iota((LAT - KL - RD, TOK), 0) == 0, owner_row, 0.0)
+    lat[c] = jnp.concatenate([lat_ref[...].astype(F32), owner_row], axis=0).T.astype(BF16)
+
+    pl.semaphore_wait(barrier, NCTX - 1 + 1 + CHIPS - 1 + 1)
+
+    half = pl.ds(pl.multiple_of(core * 128, 128), 128)
+    other_half = pl.ds(pl.multiple_of((1 - core) * 128, 128), 128)
+    quarters = [pl.ds(pl.multiple_of(core * 128 + 64 * n, 64), 64) for n in range(2)]
+    handoff = pl.ds(pl.multiple_of(t * SH, SH), SH)
+
+    def y_copy(block, target):
+        return remote(
+            lat.at[block, half], lat.at[block, half], lat_s.at[target], lat_r.at[block], {"ctx": 4 * x_lo + target, "tp": t}
+        )
+
+    def over_copy(block, n):
+        return remote(
+            lat.at[block, quarters[n]],
+            lat.at[block, quarters[n]],
+            over_s.at[n, block],
+            over_r.at[n, block],
+            {"ctx": 4 + y, "tp": (t, across)[n]},
+        )
+
+    def ext_copy(source, target):
+        return remote(
+            lat.at[c, handoff], ext.at[core, source], ext_s.at[target], ext_r.at[source], {"ctx": target, "tp": t}
+        )
+
+    def whole(source):
+        return ((x_lo == 0) & (source < 4)) | ((x_lo == 1) & (source <= c))
+
+    def ext_relay(source, whose):
+        return remote(
+            ext.at[whose, source], ext.at[whose, source], hand_s.at[source], hand_r.at[source], sibling
+        )
+
+    def cache_relay(whose):
+        return remote(cache.at[whose], cache.at[whose], cache_s, cache_r, sibling)
+
+    def relay_copy(source):
+        return remote(lat.at[source, half], lat.at[source, half], rel_s.at[source], rel_r.at[source], sibling)
+
+    def relay_arrival(source):
+        return remote(
+            lat.at[source, other_half], lat.at[source, other_half], rel_s.at[source], rel_r.at[source], sibling
+        )
+
+    @pl.when(x_lo == 0)
+    def _():
+        over_copy(c, 0).start()
+        over_copy(c, 1).start()
+
+    for d in (1, 3, 2):
+        target = (y + d) % 4
+
+        @pl.when((x_lo == 0) | (target > y))
+        def _(target=target):
+            y_copy(c, target).start()
+
     kv_loads = []
     for h in range(HD):
         for part, held in enumerate((wk, wv)):
@@ -121,82 +183,31 @@
     cache_load = pltpu.make_async_copy(cache_in, cache.at[core], load_sem.at[0])
     cache_load.start()
 
-    owner_row = jnp.broadcast_to(owner_ref[...].astype(F32).reshape(1, TOK), (LAT - KL - RD, TOK))
-    owner_row = jnp.where(iota((LAT - KL - RD, TOK), 0) == 0, owner_row, 0.0)
-    lat[c] = jnp.concatenate([lat_ref[...].astype(F32), owner_row], axis=0).T.astype(BF16)
-
-    pl.semaphore_wait(barrier, NCTX - 1 + 1 + CHIPS - 1 + 1)
-
-    half = pl.ds(pl.multiple_of(core * 128, 128), 128)
-    other_half = pl.ds(pl.multiple_of((1 - core) * 128, 128), 128)
-    quarters = [pl.ds(pl.multiple_of(core * 128 + 64 * n, 64), 64) for n in range(2)]
-    handoff = pl.ds(pl.multiple_of(t * SH, SH), SH)
-
-    def y_copy(block, target):
-        return remote(
-            lat.at[block, half], lat.at[block, half], lat_s.at[target], lat_r.at[block], {"ctx": 4 * x_lo + target, "tp": t}
-        )
-
-    def over_copy(block, n):
-        return remote(
-            lat.at[block, quarters[n]],
-            lat.at[block, quarters[n]],
-            over_s.at[n, block],
-            over_r.at[n, block],
-            {"ctx": 4 + y, "tp": (t, across)[n]},
-        )
-
-    def ext_copy(source, target):
-        return remote(
-            lat.at[c, handoff], ext.at[core, source], ext_s.at[target], ext_r.at[source], {"ctx": target, "tp": t}
-        )
-
-    def ext_relay(whose):
-        return remote(ext.at[whose], ext.at[whose], ext_s.at[NCTX], ext_r.at[NCTX], sibling)
-
-    def cache_relay(whose):
-        return remote(cache.at[whose], cache.at[whose], cache_s, cache_r, sibling)
-
-    def relay_copy(source):
-        return remote(lat.at[source, half], lat.at[source, half], rel_s.at[source], rel_r.at[source], sibling)
-
-    def relay_arrival(source):
-        return remote(
-            lat.at[source, other_half], lat.at[source, other_half], rel_s.at[source], rel_r.at[source], sibling
-        )
-
-    @pl.when(x_lo == 0)
-    def _():
-        over_copy(c, 0).start()
-        over_copy(c, 1).start()
-
-    for d in (1, 3, 2):
-        target = (y + d) % 4
-
-        @pl.when((x_lo == 0) | (target > y))
-        def _(target=target):
-            y_copy(c, target).start()
 
     def send_handoff(n, carry):
-        @pl.when(n != c)
+        @pl.when((x_lo == 1) & (n < c))
         def _():
             ext_copy(c, n).start()
 
         return carry
 
-    ext[core, c] = lat[c, handoff]
     cache_load.wait()
     cache_relay(core).start()
 
-    step_query = sq_ref[...]
+    for load in xq_loads:
+        load.wait()
+    xq[TOK:] = jnp.concatenate([sq_ref[...].astype(F32), jnp.zeros((ROWB, QL), F32)], axis=0).astype(BF16)
     nopes, ropes = [], []
     for n in range(2):
         wq_loads[n].wait()
-        up = dot(step_query, wq[n]).astype(BF16).astype(F32)
+        up = dot(xq[...], wq[n])
         for m in range(2):
-            for nope, rope in split_pair(up[:, 384 * m : 384 * (m + 1)]):
-                nopes.append(nope)
-                ropes.append(rope)
+            for e, (nope, rope) in enumerate(split_pair(up[:, 384 * m : 384 * (m + 1)])):
+                q[4 * n + 2 * m + e, :128] = nope[:TOK].T.astype(BF16)
+                q[4 * n + 2 * m + e, 128:] = rope[:TOK].T.astype(BF16)
+                nopes.append(nope[TOK : TOK + ROWB])
+                ropes.append(rope[TOK : TOK + ROWB])
+
     for load in kv_loads:
         load.wait()
     absorbed = jnp.concatenate(
@@ -231,27 +242,12 @@
             over_copy(block, 0).start()
             over_copy(block, 1).start()
 
-            @pl.when(block < c)
-            def _():
-                relay_copy(block).start()
+            relay_copy(block).start()
 
     hand_on(1)
 
-    for load in xq_loads:
-        load.wait()
-    for n in range(2):
-        up = dot(xq[...], wq[n])
-        for m in range(2):
-            for e, (nope, rope) in enumerate(split_pair(up[:, 384 * m : 384 * (m + 1)])):
-                q[4 * n + 2 * m + e, :128] = nope.T.astype(BF16)
-                q[4 * n + 2 * m + e, 128:] = rope.T.astype(BF16)
-
+    wv_t[...] = wv[...].T
     hand_on(3)
-    key_across(opposite).wait_recv()
-    for d in (1, 3, 2):
-        key_copy(opposite, d, 3 + d).start()
-    wv_t[...] = wv[...].T
-    hand_on(2)
 
     column = iota((TOK, TOK), 1)
     parity = jnp.where(column < 128, 1 - core, core)
@@ -299,8 +295,6 @@
             late = (h, raised.reshape(TOK, TOK).astype(BF16), shrink)
         weigh(*late)
 
-    fold(c, True)
-
     def forward(block):
         @pl.when(block >= 4)
         def _():
@@ -313,23 +307,54 @@
 
         relay_copy(block).start()
 
+    def block_at(n):
+        m = n - y - 1
+        other_ring = (y + m + (m // 2) * (1 - 2 * (m % 2)) + 8) % 4
+        return jnp.where((x_lo == 0) | (n <= y), c - n, other_ring)
+
+    @pl.when(x_lo == 1)
+    def _():
+        forward(block_at(1))
+
+    fold(c, True)
+    hand_on(2)
+    key_across(opposite).wait_recv()
+    for d in (1, 3, 2):
+        key_copy(opposite, d, 3 + d).start()
+
     def relay_handoff():
         def one(n, carry):
-            @pl.when(n != c)
+            @pl.when(jnp.logical_not(whole(n)))
             def _():
                 ext_copy(n, c).wait_recv()
+                ext_relay(n, core).start()
 
             return carry
 
         lax.fori_loop(0, NCTX, one, 0)
-        ext_relay(core).start()
 
     def decode():
         for side in range(2):
             for d in range(1, 4):
                 whose = 4 * (x_hi if side == 0 else 1 - x_hi) + (z + d) % 4
                 key_copy(whose, d, d).wait_recv()
-        ext_relay(1 - core).wait_recv()
+        def gather(n, carry):
+            @pl.when((x_lo == 0) & (n > c) & (n < 4))
+            def _():
+                relay_arrival(n).wait_recv()
+
+            @pl.when(whole(n))
+            def _():
+                for whose in range(2):
+                    ext[whose, n] = lat[n, pl.ds(pl.multiple_of((2 * chip + whose) * SH, SH), SH)]
+
+            @pl.when(jnp.logical_not(whole(n)))
+            def _():
+                ext_relay(n, 1 - core).wait_recv()
+
+            return carry
+
+        lax.fori_loop(0, NCTX, gather, 0)
         cache_relay(1 - core).wait_recv()
         extra = ext[...].reshape(2 * NCTX * SH, LAT)
         cached = cache[...].reshape(2 * ROWB * CPOS, KL + RD)
@@ -350,7 +375,7 @@
         sub = iota((64, 128), 0)
 
         def chunk(g):
-            query = keys[2 * g : 2 * g + 2].reshape(128, LAT)
+            query = keys[4 * g : 4 * g + 4].reshape(256, LAT)
             scores = jnp.concatenate(
                 [
                     dot_t(query[:, :KL], cached[:, :KL]) + dot_t(query[:, KL : KL + RD], cached[:, KL:]),
@@ -358,19 +383,19 @@
                 ],
                 axis=1,
             )
-            scores = (scores.reshape(16, ROWB, 768) * EXP_SCALE + bias[None]).reshape(128, 768)
+            scores = (scores.reshape(32, ROWB, 768) * EXP_SCALE + bias[None]).reshape(256, 768)
             top = jnp.max(scores, axis=1, keepdims=True)
             raised = jnp.exp2(scores - top)
             total = jnp.sum(raised, axis=1, keepdims=True)
             weights = raised.astype(BF16)
             mixed = dot(weights[:, :512], cached[:, :KL]) + dot(weights[:, 512:], extra[:, :KL])
-            acc_send[2 * g : 2 * g + 2] = mixed.astype(BF16).reshape(2, 64, KL)
-            for n in range(2):
+            acc_send[4 * g : 4 * g + 4] = mixed.astype(BF16).reshape(4, 64, KL)
+            for n in range(4):
                 rows = slice(64 * n, 64 * (n + 1))
                 packed = jnp.where(lane == sub, top[rows], 0.0) + jnp.where(lane == sub + 64, total[rows], 0.0)
-                ml_send[2 * g + n] = jnp.broadcast_to(jnp.sum(packed, axis=0, keepdims=True), (8, 128))
-
-        for g in range(4):
+                ml_send[4 * g + n] = jnp.broadcast_to(jnp.sum(packed, axis=0, keepdims=True), (8, 128))
+
+        for g in range(2):
             chunk(g)
 
         def send(d, carry):
@@ -403,16 +428,11 @@
     def ml_arrival(source):
         return remote(ml_send.at[source], ml_recv.at[source], ml_s.at[source], ml_r.at[source], sibling)
 
-    def block_at(n):
-        m = n - y - 1
-        other_ring = (y + m + (m // 2) * (1 - 2 * (m % 2)) + 8) % 4
-        return jnp.where((x_lo == 0) | (n <= y), c - n, other_ring)
-
-    @pl.when(x_lo == 1)
-    def _():
-        forward(block_at(1))
-
     def turn(n, carry):
+        @pl.when(n == 3)
+        def _():
+            relay_handoff()
+
         @pl.when((n < c) & (x_lo == 1))
         def _():
             forward(block_at(n + 1))
@@ -421,15 +441,14 @@
         def _():
             block = block_at(n)
             relay_arrival(block).wait_recv()
-            fold(block, False)
-
-        @pl.when(n == 4)
-        def _():
-            relay_handoff()
-
-        @pl.when(n == 5)
+
+        @pl.when(n == jnp.where(x_lo == 1, c, NCTX - 1))
         def _():
             decode()
+
+        @pl.when(n <= c)
+        def _():
+            fold(block_at(n), False)
 
         return carry
 
@@ -450,6 +469,9 @@
 
     def z_device(other):
         return {"ctx": c, "tp": 8 * x_hi + 2 * other + core}
+
+    def z_first(n):
+        return n % 2 == 1
 
     def x_copy(n):
         return remote(stage.at[n, there_rows], x_recv.at[n], x_s.at[n], x_r.at[n], {"ctx": c, "tp": across})
@@ -487,12 +509,12 @@
         pair_copy(n).wait_recv()
         both = (own[n].astype(F32) + pair_recv[n].astype(F32)).astype(BF16)
 
-        @pl.when(n % 2 == 0)
+        @pl.when(jnp.logical_not(z_first(n)))
         def _():
             stage[n] = both
             x_copy(n).start()
 
-        @pl.when(n % 2 == 1)
+        @pl.when(z_first(n))
         def _():
             for other in range(4):
                 for side in range(2):
@@ -502,7 +524,7 @@
                 first_z_copy(n, (z + d) % 4).start()
 
     def add_chips(n):
-        @pl.when(n % 2 == 0)
+        @pl.when(jnp.logical_not(z_first(n)))
         def _():
             x_copy(n).wait_recv()
             x_sum[n] = (stage[n, here_rows].astype(F32) + x_recv[n].astype(F32)).astype(BF16)
@@ -510,7 +532,7 @@
                 z_copy(n, (z + d) % 4).start()
             z_recv[n, z] = x_sum[n, row_block(z)]
 
-        @pl.when(n % 2 == 1)
+        @pl.when(z_first(n))
         def _():
             summed = stage[n, row_block(z, 2 * SH)].astype(F32)
             for d in (1, 3, 2):
@@ -566,26 +588,37 @@
             mixed[ROWB * h : ROWB * (h + 1)].astype(BF16), wv[:, 128 * h : 128 * (h + 1)]
         )
 
+    def sum_z(n):
+        for d in range(1, 4):
+            z_arrival(n, (z + d) % 4).wait_recv()
+        summed = z_recv[n, 0].astype(F32)
+        for other in range(1, 4):
+            summed = summed + z_recv[n, other].astype(F32)
+        out_ref[:, CW * n : CW * (n + 1)] = summed
+
+    def sum_x(n):
+        last_x_copy(n).wait_recv()
+        summed = x_sum[n, row_block(x_hi)].astype(F32) + x_recv[n, :SH].astype(F32)
+        out_ref[:, CW * n : CW * (n + 1)] = summed
+
     for n in range(NCH):
-        if n % 2 == 0:
-            for d in range(1, 4):
-                z_arrival(n, (z + d) % 4).wait_recv()
-            summed = z_recv[n, 0].astype(F32)
-            for other in range(1, 4):
-                summed = summed + z_recv[n, other].astype(F32)
+        if z_first(n):
+            sum_x(n)
         else:
-            last_x_copy(n).wait_recv()
-            summed = x_sum[n, row_block(x_hi)].astype(F32) + x_recv[n, :SH].astype(F32)
-        out_ref[:, CW * n : CW * (n + 1)] = summed
+            sum_z(n)
 
     def drain_ctx(n, carry):
-        @pl.when(n < c)
+        @pl.when((n != c) & whole(n))
         def _():
             relay_copy(n).wait_send()
 
-        @pl.when(n != c)
+        @pl.when((x_lo == 1) & (n < c))
         def _():
             ext_copy(c, n).wait_send()
+
+        @pl.when(jnp.logical_not(whole(n)))
+        def _():
+            ext_relay(n, core).wait_send()
 
         @pl.when(n != chip)
         def _():
@@ -613,19 +646,18 @@
     for d in (1, 3, 2):
         key_copy(chip, d, d).wait_send()
         key_copy(opposite, d, 3 + d).wait_send()
-    ext_relay(core).wait_send()
     cache_relay(core).wait_send()
 
     def drain_columns(n, carry):
         pair_copy(n).wait_send()
 
-        @pl.when(n % 2 == 0)
+        @pl.when(jnp.logical_not(z_first(n)))
         def _():
             x_copy(n).wait_send()
             for d in range(1, 4):
                 z_copy(n, (z + d) % 4).wait_send()
 
-        @pl.when(n % 2 == 1)
+        @pl.when(z_first(n))
         def _():
             last_x_copy(n).wait_send()
             for d in range(1, 4):
@@ -668,7 +700,7 @@
         scratch_shapes=[
             vmem((NCTX, TOK, LAT), BF16),
             vmem((2, NCTX, SH, LAT), BF16),
-            vmem((TOK, QL), BF16),
+            vmem((TOK + 2 * ROWB, QL), BF16),
             vmem((2, QL, 768), BF16),
             vmem((KL, HD * NOPE), BF16),
             vmem((KL, HD * VD), BF16),
@@ -704,8 +736,10 @@
             dma((2, 4)),
             dma((NCTX,)),
             dma((NCTX,)),
-            dma((NCTX + 1,)),
-            dma((NCTX + 1,)),
+            dma((NCTX,)),
+            dma((NCTX,)),
+            dma((NCTX,)),
+            dma((NCTX,)),
             dma,
             dma,
             dma((CHIPS,)),

time: 64.1 us -> 60.9 us (0.950)
  the two profiles are of different devices: /device:TPU:6 before, /device:TPU:26 now
where the time goes in v4:
time: 60.9 us; the launch traced here: 60.8 us
  Pallas kernels  60.1 us (99%)
  between operations  0.64 us (1%)
    pallas_call x1, Pallas kernels, body(): pl.pallas_call(kernel, out_shape=out_shape, in_specs=[in_vmem] * 2 + [any...  58.3 us
    pallas_call x1, Pallas kernels, body(): pl.pallas_call(place, out_shape=out_shape, in_specs=[in_vmem] * 2, out_sp...  1.82 us

profile of v4, /device:TPU:26, one launch (start us, length us, event | category | flops | bytes accessed | tf_op | source)
XLA Modules:
  0.0 60.8 jit_solution(6883383912916265901)
XLA Ops:
  0.6 58.3 %attention.1 = (f32[16,7168]{1,0:T(8,128)}, f32[8,1024]{1,0:T(8,128)}) custom-call(bf16[576,256]{1,0:T(8,128)(2,1)} %bitcast.3, s32[256]{0:T(256)} %owner_ref.1, bf16[256,1536]{1,0:T(8,128)(2,1)} %xq_in.1, bf16[1536,1536]{1,0:T(8,128)(2,1)} %wq_in.1, bf16[512,2048]{1,0:T(8,128)(2,1)} %kv_in.1, bf16[1024,7168]{1,0:T(8,128)(2,1)} %wo_in.1, ...), custom_call_target="tpu_custom_call" | custom-call | tf_op jit(solution)/shard_map/attention/pallas_call | solution.py:695
  59.0 1.8 %place.1 = (f32[16,7168]{1,0:T(8,128)}, f32[8,1024]{1,0:T(8,128)}) custom-call(f32[16,7168]{1,0:T(8,128)} %get-tuple-element.4.span_in, f32[8,1024]{1,0:T(8,128)} %get-tuple-element.5.step_in), custom_call_target="tpu_custom_call" | custom-call | tf_op jit(solution)/shard_map/place/pallas_call | solution.py:773

commit v5 on v4

--- a/solution.py
+++ b/solution.py
@@ -57,9 +57,9 @@
 
 
 def kernel(
-    lat_ref, owner_ref, xq_in, wq_in, kv_in, wo_in, sq_ref, cache_in, len_ref,
+    lat_in, owner_in, xq_in, wq_in, kv_in, wo_in, sq_in, cache_in, len_in,
     out_ref, step_ref,
-    lat, ext, xq, wq, wk, wv, wv_t, wo, cache, q, run_max, run_sum, run_acc, head_out,
+    lat_ref, owner_ref, sq_ref, len_ref, lat, ext, xq, wq, wk, wv, wv_t, wo, cache, q, run_max, run_sum, run_acc, head_out,
     keys, acc_send, acc_recv, ml_send, ml_recv,
     pair_send, own, pair_recv, stage, x_recv, x_sum, z_recv, zz_recv,
     load_sem, kv_sem, wq_sem, wo_sem, xq_sem,
@@ -83,6 +83,14 @@
             src_ref=src, dst_ref=dst, send_sem=send, recv_sem=recv, device_id=device, device_id_type=MESH
         )
 
+    small_loads = [
+        pltpu.make_async_copy(source, held, load_sem.at[1 + n])
+        for n, (source, held) in enumerate(
+            ((lat_in, lat_ref), (owner_in, owner_ref), (sq_in, sq_ref), (len_in, len_ref))
+        )
+    ]
+    for load in small_loads:
+        load.start()
     wq_loads = [
         pltpu.make_async_copy(wq_in.at[:, pl.ds(768 * n, 768)], wq.at[n], wq_sem.at[n]) for n in range(2)
     ]
@@ -97,6 +105,8 @@
         pl.semaphore_signal(barrier, inc=1, device_id={"ctx": c, "tp": (t + 2 * d) % NTP}, device_id_type=MESH)
     pl.semaphore_signal(barrier, inc=1, device_id=sibling, device_id_type=MESH)
 
+    for load in small_loads:
+        load.wait()
     owner_row = jnp.broadcast_to(owner_ref[...].astype(F32).reshape(1, TOK), (LAT - KL - RD, TOK))
     owner_row = jnp.where(iota((LAT - KL - RD, TOK), 0) == 0, owner_row, 0.0)
     lat[c] = jnp.concatenate([lat_ref[...].astype(F32), owner_row], axis=0).T.astype(BF16)
@@ -317,6 +327,15 @@
         forward(block_at(1))
 
     fold(c, True)
+
+    early = (x_lo == 1) & (y >= 1)
+    ahead = jnp.where(early, 2, 1)
+    decode_turn = jnp.where(x_lo == 1, c + 1 - ahead, NCTX - 1)
+
+    @pl.when(early)
+    def _():
+        forward(block_at(2))
+
     hand_on(2)
     key_across(opposite).wait_recv()
     for d in (1, 3, 2):
@@ -433,17 +452,20 @@
         def _():
             relay_handoff()
 
-        @pl.when((n < c) & (x_lo == 1))
-        def _():
-            forward(block_at(n + 1))
-
-        @pl.when(n <= c)
-        def _():
-            block = block_at(n)
-            relay_arrival(block).wait_recv()
-
-        @pl.when(n == jnp.where(x_lo == 1, c, NCTX - 1))
-        def _():
+        @pl.when((n + ahead <= c) & (x_lo == 1))
+        def _():
+            forward(block_at(n + ahead))
+
+        @pl.when((n <= c) & jnp.logical_not(early & (n == c)))
+        def _():
+            relay_arrival(block_at(n)).wait_recv()
+
+        @pl.when(n == decode_turn)
+        def _():
+            @pl.when(early)
+            def _():
+                relay_arrival(block_at(c)).wait_recv()
+
             decode()
 
         @pl.when(n <= c)
@@ -695,9 +717,13 @@
     results = pl.pallas_call(
         kernel,
         out_shape=out_shape,
-        in_specs=[in_vmem] * 2 + [anywhere] * 4 + [in_vmem, anywhere, pl.BlockSpec(memory_space=pltpu.SMEM)],
+        in_specs=[anywhere] * 9,
         out_specs=(in_vmem, in_vmem),
         scratch_shapes=[
+            vmem((KL + RD, TOK), BF16),
+            vmem((TOK,), jnp.int32),
+            vmem((ROWB, QL), BF16),
+            pltpu.SMEM((ROWB,), jnp.int32),
             vmem((NCTX, TOK, LAT), BF16),
             vmem((2, NCTX, SH, LAT), BF16),
             vmem((TOK + 2 * ROWB, QL), BF16),
@@ -725,7 +751,7 @@
             vmem((NCH, 64, CW), BF16),
             vmem((NCH, 4, SH, CW), BF16),
             vmem((NCH, 4, 2 * SH, CW), BF16),
-            dma((1,)),
+            dma((5,)),
             dma((2, HD)),
             dma((2,)),
             dma((NCH,)),

time: 60.9 us -> 59.1 us (0.970)
  Pallas kernels: 60.1 us -> 58.3 us
    pallas_call x1, Pallas kernels: 58.3 us -> 56.5 us  [body(): pl.pallas_call(kernel, out_shape=out_shape, in_specs=[anywhere] * 9, out_...]
where the time goes in v5:
time: 59.1 us; the launch traced here: 58.9 us
  Pallas kernels  58.3 us (99%)
  between operations  0.64 us (1%)
    pallas_call x1, Pallas kernels, body(): pl.pallas_call(kernel, out_shape=out_shape, in_specs=[anywhere] * 9, out_...  56.5 us
    pallas_call x1, Pallas kernels, body(): pl.pallas_call(place, out_shape=out_shape, in_specs=[in_vmem] * 2, out_sp...  1.82 us

profile of v5, /device:TPU:26, one launch (start us, length us, event | category | flops | bytes accessed | tf_op | source)
XLA Modules:
  0.0 58.9 jit_solution(7718190798401440185)
XLA Ops:
  0.6 56.5 %attention.1 = (f32[16,7168]{1,0:T(8,128)}, f32[8,1024]{1,0:T(8,128)}) custom-call(bf16[576,256]{1,0:T(8,128)(2,1)} %bitcast.3, s32[256]{0:T(256)} %owner_in.1, bf16[256,1536]{1,0:T(8,128)(2,1)} %xq_in.1, bf16[1536,1536]{1,0:T(8,128)(2,1)} %wq_in.1, bf16[512,2048]{1,0:T(8,128)(2,1)} %kv_in.1, bf16[1024,7168]{1,0:T(8,128)(2,1)} %wo_in.1, ...), custom_call_target="tpu_custom_call" | custom-call | tf_op jit(solution)/shard_map/attention/pallas_call | solution.py:717
  57.1 1.8 %place.1 = (f32[16,7168]{1,0:T(8,128)}, f32[8,1024]{1,0:T(8,128)}) custom-call(f32[16,7168]{1,0:T(8,128)} %get-tuple-element.4.span_in, f32[8,1024]{1,0:T(8,128)} %get-tuple-element.5.step_in), custom_call_target="tpu_custom_call" | custom-call | tf_op jit(solution)/shard_map/place/pallas_call | solution.py:799

commit v6 on v5

--- a/solution.py
+++ b/solution.py
@@ -573,13 +573,13 @@
         def _():
             add_core(n - 1)
 
-        @pl.when(n >= 3)
-        def _():
-            add_chips(n - 3)
+        @pl.when(n >= 4)
+        def _():
+            add_chips(n - 4)
 
         return carry
 
-    lax.fori_loop(0, NCH + 3, column_turn, 0)
+    lax.fori_loop(0, NCH + 4, column_turn, 0)
 
     def merge_arrivals(d, carry):
         source = (chip + d) % CHIPS

time: 59.1 us -> 56.4 us (0.954)
  Pallas kernels: 58.3 us -> 55.5 us
    pallas_call x1, Pallas kernels: 56.5 us -> 53.7 us  [body(): pl.pallas_call(kernel, out_shape=out_shape, in_specs=[anywhere] * 9, out_...]
where the time goes in v6:
time: 56.4 us; the launch traced here: 56.2 us
  Pallas kernels  55.5 us (98%)
  between operations  0.64 us (1%)
    pallas_call x1, Pallas kernels, body(): pl.pallas_call(kernel, out_shape=out_shape, in_specs=[anywhere] * 9, out_...  53.7 us
    pallas_call x1, Pallas kernels, body(): pl.pallas_call(place, out_shape=out_shape, in_specs=[in_vmem] * 2, out_sp...  1.82 us

profile of v6, /device:TPU:26, one launch (start us, length us, event | category | flops | bytes accessed | tf_op | source)
XLA Modules:
  0.0 56.2 jit_solution(950514386674021018)
XLA Ops:
  0.6 53.7 %attention.1 = (f32[16,7168]{1,0:T(8,128)}, f32[8,1024]{1,0:T(8,128)}) custom-call(bf16[576,256]{1,0:T(8,128)(2,1)} %bitcast.3, s32[256]{0:T(256)} %owner_in.1, bf16[256,1536]{1,0:T(8,128)(2,1)} %xq_in.1, bf16[1536,1536]{1,0:T(8,128)(2,1)} %wq_in.1, bf16[512,2048]{1,0:T(8,128)(2,1)} %kv_in.1, bf16[1024,7168]{1,0:T(8,128)(2,1)} %wo_in.1, ...), custom_call_target="tpu_custom_call" | custom-call | tf_op jit(solution)/shard_map/attention/pallas_call | solution.py:717
  54.4 1.8 %place.1 = (f32[16,7168]{1,0:T(8,128)}, f32[8,1024]{1,0:T(8,128)}) custom-call(f32[16,7168]{1,0:T(8,128)} %get-tuple-element.4.span_in, f32[8,1024]{1,0:T(8,128)} %get-tuple-element.5.step_in), custom_call_target="tpu_custom_call" | custom-call | tf_op jit(solution)/shard_map/place/pallas_call | solution.py:799
